TPU v7x, 128 devices: a whole 4x4x4 slice. The times are simulated.
128 devices in a mesh: space: 64 (over z, y, x_lo, core), tm: 2 (over x_hi).
Axes of the slice: x: 4 (x_hi: 2, x_lo: 2; x = x_hi * 2 + x_lo), y: 4, z: 4, core: 2. Of those that a mesh axis runs over, the one named last changes fastest.
Arguments:
- hidden: bfloat16 [2, 4, 8192, 4096], P(None, None, ('space', 'tm')), may hold values from -6 to 6
- modulation: float32 [2, 4096], replicated, may hold values from -3 to 3
- w_proj: bfloat16 [4096, 64], replicated, may hold values from -0.09375 to 0.09375
- b_proj: float32 [64], replicated, may hold values from -2 to 2
- guidance: float32 [1], replicated, may hold values from 1.5 to 3
- x_noisy: float32 [4, 256, 128, 16], P('tm', 'space'), may hold values from -6 to 6
- sigma: float32 [1], replicated, may hold values from 0.3 to 0.8
- w_in: bfloat16 [3, 3, 48, 512], replicated, may hold values from -0.3125 to 0.3125
- b_in: float32 [512], replicated, may hold values from -2 to 2
- gain: float32 [512], replicated, may hold values from 0.1 to 1.9
- w_mid: bfloat16 [3, 3, 1536, 512], replicated, may hold values from -0.0546875 to 0.0546875
- b_mid: float32 [512], replicated, may hold values from -2 to 2
- w_up: bfloat16 [3, 1536, 512], replicated, may hold values from -0.09375 to 0.09375
- b_up: float32 [512], replicated, may hold values from -2 to 2
Outputs:
- decoded: bfloat16 [4, 512, 256, 512], P('tm', 'space')
All inputs are finite; a program needn't handle non-finite values.
Results may differ from a plain program's by a relative error of at most 0.015.
Values may be sent and summed in bfloat16 or wider, within the bound.
A program may use at most 192 MiB of HBM per device.

v0:
```python
import jax
import jax.numpy as jnp
from jax import lax
from jax.sharding import PartitionSpec as P

norm_eps = 1e-06


def shifted(x, axis, by):
    size = lax.axis_size(axis)
    pairs = [(i, i + by) for i in range(size) if 0 <= i + by < size]
    return lax.ppermute(x, axis, pairs)


def padded_2(x, sides, width):
    for axis, dim in sides:
        size, length = (lax.axis_size(axis), x.shape[dim])
        up = [(i, (i + 1) % size) for i in range(size - 1)]
        down = [(j, i) for i, j in up]
        last = lax.slice_in_dim(x, length - width, length, axis=dim)
        first = lax.slice_in_dim(x, 0, width, axis=dim)
        before = lax.ppermute(last, axis, up)
        after = lax.ppermute(first, axis, down)
        x = jnp.concatenate([before, x, after], axis=dim)
    return x


def modulate(hidden, modulation):
    values = hidden.astype(jnp.float32)
    centre = jnp.mean(values, axis=-1, keepdims=True)
    spread = jnp.mean(jnp.square(values - centre), axis=-1, keepdims=True)
    normed = (values - centre) * lax.rsqrt(spread + norm_eps)
    return (normed * (1.0 + modulation[1]) + modulation[0]).astype(jnp.bfloat16)


def unpatchify(patch_rows, row_count, col_count, lat_count):
    frame_count = patch_rows.shape[0]
    patch_grid = patch_rows.reshape(frame_count, row_count // 2, col_count // 2, 2, 2, lat_count)
    return patch_grid.transpose(0, 1, 3, 2, 4, 5).reshape(
        frame_count, row_count, col_count, lat_count
    )


def apply_taps(padded, weight, frame_count, row_count, col_count):
    tap_depth = weight.shape[0]
    channels = padded.shape[-1]
    accumulated = jnp.zeros((frame_count * row_count * col_count, weight.shape[-1]), jnp.float32)
    for step_t in range(tap_depth):
        for step_h in range(3):
            block_slice = padded[step_t : step_t + frame_count, step_h : step_h + row_count]
            window = jnp.concatenate(
                [block_slice[:, :, step_w : step_w + col_count] for step_w in range(3)], axis=-1
            )
            accumulated = accumulated + jnp.dot(
                window.reshape(-1, 3 * channels),
                weight[step_t, step_h],
                preferred_element_type=jnp.float32,
            )
    return accumulated.reshape(frame_count, row_count, col_count, weight.shape[-1])


def rms_silu(values, gain):
    wide = values.astype(jnp.float32)
    inverse_rms = lax.rsqrt(jnp.mean(jnp.square(wide), axis=-1, keepdims=True) + norm_eps)
    return jax.nn.silu(wide * inverse_rms * gain).astype(jnp.bfloat16)


def causal_conv(values, weight):
    frame_count = values.shape[0]
    earlier = shifted(values, "tm", 1)
    extended = jnp.concatenate([earlier, values], axis=0)
    extended = padded_2(extended, (("space", 1),), 1)
    extended = jnp.pad(extended, ((0, 0), (0, 0), (1, 1), (0, 0)))
    return apply_taps(extended, weight, frame_count, values.shape[1], values.shape[2])


def upsample_nearest(values):
    return jnp.repeat(jnp.repeat(values, 2, axis=1), 2, axis=2)


def on_device(
    hidden,
    modulation,
    w_proj,
    b_proj,
    guidance,
    x_noisy,
    sigma,
    w_in,
    b_in,
    gain,
    w_mid,
    b_mid,
    w_up,
    b_up,
):
    modulated = modulate(hidden, modulation)
    shard_len = modulated.shape[2]
    branches = jnp.dot(
        modulated.reshape(-1, modulated.shape[-1]), w_proj, preferred_element_type=jnp.float32
    )
    branches = branches.reshape(2, modulated.shape[1], shard_len, w_proj.shape[1]) + b_proj
    cond_rows, uncond_rows = (
        lax.all_to_all(branches[0], "tm", split_axis=0, concat_axis=1, tiled=True),
        lax.all_to_all(branches[1], "tm", split_axis=0, concat_axis=1, tiled=True),
    )
    prediction = uncond_rows + guidance[0] * (cond_rows - uncond_rows)
    frame_count, row_count, col_count = (x_noisy.shape[0], x_noisy.shape[1], x_noisy.shape[2])
    velocity = unpatchify(prediction, row_count, col_count, x_noisy.shape[3])
    latent = (x_noisy - sigma[0] * velocity).astype(jnp.bfloat16)
    first_out = (causal_conv(latent, w_in) + b_in).astype(jnp.bfloat16)
    activated = rms_silu(first_out, gain)
    middle = causal_conv(activated, w_mid)
    second = (first_out.astype(jnp.float32) + middle + b_mid).astype(jnp.bfloat16)
    fine_grid = upsample_nearest(second)
    padded = padded_2(fine_grid, (("space", 1),), 1)
    padded = jnp.pad(padded, ((0, 0), (0, 0), (1, 1), (0, 0)))
    decoded = apply_taps(padded, w_up[None], frame_count, 2 * row_count, 2 * col_count) + b_up
    return decoded.astype(jnp.bfloat16)


def solution(mesh):
    return jax.shard_map(
        on_device,
        mesh=mesh,
        in_specs=(
            P(None, None, ("space", "tm"), None),
            P(),
            P(),
            P(),
            P(),
            P("tm", "space", None, None),
            P(),
            P(),
            P(),
            P(),
            P(),
            P(),
            P(),
            P(),
        ),
        out_specs=P("tm", "space", None, None),
        check_vma=False,
    )
```

profile of v0, /device:TPU:31, one launch (start us, length us, event | category | flops | bytes accessed | tf_op | source)
XLA Modules:
  0.0 285.7 jit_solution(12358617119306877787)
XLA Ops:
  0.0 3.0 %convert_reduce_fusion = f32[2,4,64]{2,1,0:T(4,128)S(1)} fusion(bf16[2,4,64,4096]{3,2,1,0:T(8,128)(2,1)} %param.14), kind=kLoop, calls=%fused_computation.16 | loop fusion | flops 4193792 | bytes 4196352 | tf_op jit(solution)/shard_map/reduce_sum | solution.py:30
  3.5 1.2 fusion.13
  4.8 1.9 fusion.67
  6.7 0.8 reshape.160
  7.5 4.4 %all-to-all-start.1 = ((f32[2,1,8192]{2,1,0:T(1,128)}), f32[2,1,8192]{2,1,0:T(1,128)S(1)}, u32[]{:S(2)}, u32[]{:S(2)}) async-start(f32[2,1,8192]{2,1,0:T(1,128)} %reshape.160), calls=%async_computation.1 | async-start | bytes 131072 | tf_op jit(solution)/shard_map/all_to_all | solution.py:104
  11.9 0.8 reshape.158
  12.6 0.8 all-to-all-done.1
  13.4 6.2 %all-to-all-start = ((f32[2,1,8192]{2,1,0:T(1,128)}), f32[2,1,8192]{2,1,0:T(1,128)S(1)}, u32[]{:S(2)}, u32[]{:S(2)}) async-start(f32[2,1,8192]{2,1,0:T(1,128)} %reshape.158), calls=%async_computation | async-start | bytes 131072 | tf_op jit(solution)/shard_map/all_to_all | solution.py:105
  21.7 0.8 reduce.2
  22.7 0.8 reduce.1
  24.0 1.3 collective-permute-start
  25.4 7.6 %collective-permute-done = bf16[2,4,128,16]{3,2,1,0:T(8,128)(2,1)S(1)} collective-permute-done((bf16[2,4,128,16]{3,2,1,0:T(8,128)(2,1)S(1)}, bf16[2,4,128,16]{3,2,1,0:T(8,128)(2,1)S(1)}, u32[]{:S(2)}, u32[]{:S(2)}) %collective-permute-start) | collective-permute-done | bytes 32800 | tf_op jit(solution)/shard_map/ppermute | solution.py:12
  33.2 6.3 %collective-permute-start.1 = (bf16[4,1,128,16]{2,3,1,0:T(8,128)(2,1)S(1)}, bf16[4,1,128,16]{2,3,1,0:T(8,128)(2,1)S(1)}, u32[]{:S(2)}, u32[]{:S(2)}) collective-permute-start(bf16[4,1,128,16]{2,3,1,0:T(8,128)(2,1)S(1)} %get-tuple-element.74), channel_id=1, source_target_pairs={{0,2},{2,4},{4,6},{6,8},{8,10},{10,12},{12,14},{14,16},{16,18},{18... | collective-permute-start | bytes 49160 | tf_op jit(solution)/shard_map/ppermute | solution.py:22
  39.5 2.4 collective-permute-start.2
  42.0 0.9 copy.92
  42.8 4.7 %collective-permute-done.2 = bf16[4,1,128,16]{2,3,1,0:T(8,128)(2,1)S(1)} collective-permute-done((bf16[4,1,128,16]{2,3,1,0:T(8,128)(2,1)S(1)}, bf16[4,1,128,16]{2,3,1,0:T(8,128)(2,1)S(1)}, u32[]{:S(2)}, u32[]{:S(2)}) %collective-permute-start.2) | collective-permute-done | bytes 16416 | tf_op jit(solution)/shard_map/ppermute | solution.py:23
  48.0 1.6 pad_slice_fusion.15
  49.5 1.5 pad_slice_fusion.17
  51.1 0.9 copy.85
  52.0 0.9 copy.96
  53.0 0.9 copy.94
  53.9 0.8 copy.99
  54.7 0.8 copy.88
  55.6 1.5 pad_maximum_fusion.19
  57.1 1.2 fusion.79
  63.4 1.7 multiply_reduce_fusion
  65.2 0.7 fusion.36
  65.8 1.3 collective-permute-start.3
  67.1 23.1 %collective-permute-done.3 = bf16[2,4,128,512]{3,2,1,0:T(8,128)(2,1)S(1)} collective-permute-done((bf16[2,4,128,512]{3,2,1,0:T(8,128)(2,1)S(1)}, bf16[2,4,128,512]{3,2,1,0:T(8,128)(2,1)S(1)}, u32[]{:S(2)}, u32[]{:S(2)}) %collective-permute-start.3) | collective-permute-done | bytes 1048608 | tf_op jit(solution)/shard_map/ppermute | solution.py:12
  90.4 4.4 %collective-permute-start.4 = (bf16[4,1,128,512]{3,2,1,0:T(8,128)(2,1)S(1)}, bf16[4,1,128,512]{3,2,1,0:T(8,128)(2,1)S(1)}, u32[]{:S(2)}, u32[]{:S(2)}) collective-permute-start(bf16[4,1,128,512]{3,2,1,0:T(8,128)(2,1)S(1)} %get-tuple-element.41), channel_id=1, source_target_pairs={{0,2},{2,4},{4,6},{6,8},{8,10},{10,12},{12,14},{14,16},{16,18},{18... | collective-permute-start | bytes 1572872 | tf_op jit(solution)/shard_map/ppermute | solution.py:22
  94.7 2.1 collective-permute-start.5
  96.8 8.8 %collective-permute-done.4 = bf16[4,1,128,512]{3,2,1,0:T(8,128)(2,1)S(1)} collective-permute-done((bf16[4,1,128,512]{3,2,1,0:T(8,128)(2,1)S(1)}, bf16[4,1,128,512]{3,2,1,0:T(8,128)(2,1)S(1)}, u32[]{:S(2)}, u32[]{:S(2)}) %collective-permute-start.4) | collective-permute-done | bytes 524320 | tf_op jit(solution)/shard_map/ppermute | solution.py:22
  105.6 2.6 collective-permute-done.5
  108.9 1.8 fusion.103
  110.7 1.8 fusion.104
  112.4 2.0 select_maximum_fusion
  114.4 7.6 %fusion.102 = (bf16[2,4,128,512]{3,2,1,0:T(8,128)(2,1)S(1)}, bf16[2,4,128,512]{3,2,1,0:T(8,128)(2,1)S(1)}, bf16[2,4,128,512]{3,2,1,0:T(8,128)(2,1)S(1)}, bf16[2,...) fusion(bf16[4,6,130,512]{3,2,1,0:T(8,128)(2,1)S(1)} %select_max, ...), kind=kLoop, calls=%fused_computation.173 | loop fusion | bytes 37748736 | tf_op jit(solution)/shard_map/slice | solution.py:52
  122.0 2.0 pad_maximum_fusion.8
  124.1 4.7 %fusion.44 = f32[1024,512]{1,0:T(8,128)} fusion(bf16[1024,1536]{1,0:T(8,128)(2,1)S(1)} %bitcast.151, bf16[3,3,1536,512]{3,2,1,0:T(8,128)(2,1)} %param.24), kind=kOutput, calls=%fused_computation.76 | convolution fusion | flops 1610612736 | bytes 6815744 | tf_op jit(solution)/shard_map/dot_general | solution.py:54
  129.1 4.7 %fusion.46 = f32[1024,512]{1,0:T(8,128)} fusion(bf16[1024,1536]{1,0:T(8,128)(2,1)S(1)} %bitcast.152, bf16[3,3,1536,512]{3,2,1,0:T(8,128)(2,1)} %param.24), kind=kOutput, calls=%fused_computation.78 | convolution fusion | flops 1610612736 | bytes 6815744 | tf_op jit(solution)/shard_map/dot_general | solution.py:54
  134.1 4.7 %fusion.50 = f32[1024,512]{1,0:T(8,128)} fusion(bf16[1024,1536]{1,0:T(8,128)(2,1)S(1)} %bitcast.153, bf16[3,3,1536,512]{3,2,1,0:T(8,128)(2,1)} %param.24), kind=kOutput, calls=%fused_computation.82 | convolution fusion | flops 1610612736 | bytes 6815744 | tf_op jit(solution)/shard_map/dot_general | solution.py:54
  139.1 4.7 %fusion.52 = f32[1024,512]{1,0:T(8,128)} fusion(bf16[1024,1536]{1,0:T(8,128)(2,1)S(1)} %bitcast.154, bf16[3,3,1536,512]{3,2,1,0:T(8,128)(2,1)} %param.24), kind=kOutput, calls=%fused_computation.84 | convolution fusion | flops 1610612736 | bytes 6815744 | tf_op jit(solution)/shard_map/dot_general | solution.py:54
  144.0 4.6 %fusion.56 = f32[1024,512]{1,0:T(8,128)} fusion(bf16[1024,1536]{1,0:T(8,128)(2,1)S(1)} %bitcast.155, bf16[3,3,1536,512]{3,2,1,0:T(8,128)(2,1)} %param.24), kind=kOutput, calls=%fused_computation.88 | convolution fusion | flops 1610612736 | bytes 6815744 | tf_op jit(solution)/shard_map/dot_general | solution.py:54
  148.6 0.9 pad_maximum_fusion.4
  149.6 3.2 %fusion.54 = f32[1024,512]{1,0:T(8,128)S(1)} fusion(bf16[1024,1536]{1,0:T(8,128)(2,1)S(1)} %bitcast.158, bf16[3,3,1536,512]{3,2,1,0:T(8,128)(2,1)} %param.24), kind=kOutput, calls=%fused_computation.86 | convolution fusion | flops 1610612736 | bytes 6815744 | tf_op jit(solution)/shard_map/dot_general | solution.py:54
  152.8 4.6 %fusion.48 = f32[1024,512]{1,0:T(8,128)} fusion(bf16[1024,1536]{1,0:T(8,128)(2,1)S(1)} %bitcast.157, bf16[3,3,1536,512]{3,2,1,0:T(8,128)(2,1)} %param.24), kind=kOutput, calls=%fused_computation.80 | convolution fusion | flops 1610612736 | bytes 6815744 | tf_op jit(solution)/shard_map/dot_general | solution.py:54
  157.4 4.7 %fusion.42 = f32[1024,512]{1,0:T(8,128)} fusion(bf16[1024,1536]{1,0:T(8,128)(2,1)S(1)} %bitcast.156, bf16[3,3,1536,512]{3,2,1,0:T(8,128)(2,1)} %param.24), kind=kOutput, calls=%fused_computation.74 | convolution fusion | flops 1610612736 | bytes 6815744 | tf_op jit(solution)/shard_map/dot_general | solution.py:54
  162.6 1.0 copy-done.17
  164.2 0.6 copy-done.19
  164.9 5.2 %add_add_fusion.1 = f32[1024,512]{1,0:T(8,128)S(1)} fusion(f32[1024,512]{1,0:T(8,128)} %fusion.42, f32[1024,512]{1,0:T(8,128)S(1)} %copy-done.17, f32[1024,512]{1,0:T(8,128)S(1)} %copy-done.18, f32[1024,512]{1,0:T(8,128)} %fusion.48, f32[1024,512]{1,0:T(8,128)S(1)} %copy-done.19, f32[1024,512]{1,0:T(8,128)S(1)} %copy-done.20, ...), kind=kOutput, calls=%fused_computation.63 | convolution fusion | flops 1614807040 | bytes 23592960 | tf_op jit(solution)/shard_map/dot_general | solution.py:54
  170.9 3.5 %broadcast_in_dim.7 = bf16[2,8,128,2,512]{4,3,2,1,0:T(2,128)(2,1)} broadcast(bf16[2,8,128,512]{3,2,1,0:T(8,128)(2,1)S(1)} %bitcast.147), dimensions={0,1,2,4} | broadcast | bytes 6291456 | tf_op jit(solution)/shard_map/broadcast_in_dim | solution.py:78
  174.5 7.3 %reshape.153 = bf16[2,8,256,512]{3,2,1,0:T(8,128)(2,1)} reshape(bf16[2,8,128,2,512]{4,3,2,1,0:T(2,128)(2,1)} %broadcast_in_dim.7) | data formatting | bytes 8388608 | tf_op jit(solution)/shard_map/reshape | solution.py:78
  181.7 1.3 fusion.101
  183.0 1.9 collective-permute-start.7
  184.9 6.7 %collective-permute-start.6 = (bf16[2,1,256,512]{3,2,1,0:T(8,128)(2,1)S(1)}, bf16[2,1,256,512]{3,2,1,0:T(8,128)(2,1)S(1)}, u32[]{:S(2)}, u32[]{:S(2)}) collective-permute-start(bf16[2,1,256,512]{3,2,1,0:T(8,128)(2,1)S(1)} %get-tuple-element.14), channel_id=1, source_target_pairs={{0,2},{2,4},{4,6},{6,8},{8,10},{10,12},{12,14},{14,16},{16,18},{18... | collective-permute-start | bytes 1572872 | tf_op jit(solution)/shard_map/ppermute | solution.py:22
  191.6 7.2 %concatenate.141 = bf16[4096,512]{1,0:T(8,128)(2,1)} reshape(bf16[2,8,128,2,512]{4,3,2,1,0:T(2,128)(2,1)} %broadcast_in_dim.7) | data formatting | bytes 8388608 | tf_op jit(solution)/shard_map/concatenate | solution.py:51
  198.8 3.3 %collective-permute-done.7 = bf16[2,1,256,512]{3,2,1,0:T(8,128)(2,1)S(1)} collective-permute-done((bf16[2,1,256,512]{3,2,1,0:T(8,128)(2,1)S(1)}, bf16[2,1,256,512]{3,2,1,0:T(8,128)(2,1)S(1)}, u32[]{:S(2)}, u32[]{:S(2)}) %collective-permute-start.7) | collective-permute-done | bytes 524320 | tf_op jit(solution)/shard_map/ppermute | solution.py:23
  202.1 7.2 %fusion.22 = bf16[2,10,258,512]{3,2,1,0:T(8,128)(2,1)} fusion(bf16[2,1,256,512]{3,2,1,0:T(8,128)(2,1)S(1)} %collective-permute-done.7, bf16[2,8,256,512]{3,2,1,0:T(8,128)(2,1)} %reshape.153, bf16[2,1,256,512]{3,2,1,0:T(8,128)(2,1)S(1)} %collective-permute-done.6), kind=kLoop, calls=%fused_computation.32 | loop fusion | flops 31703040 | bytes 10526720 | tf_op jit(solution)/shard_map/concatenate | solution.py:24
  209.3 17.5 %fusion.100 = (bf16[2,8,256,512]{3,2,1,0:T(8,128)(2,1)}, bf16[2,8,256,512]{3,2,1,0:T(8,128)(2,1)}, bf16[2,8,256,512]{3,2,1,0:T(8,128)(2,1)}, bf16[2,8,256,512]{3...) fusion(bf16[2,10,258,512]{3,2,1,0:T(8,128)(2,1)} %fusion.22), kind=kLoop, calls=%fused_computation.171 | loop fusion | bytes 50331648 | tf_op jit(solution)/shard_map/slice | solution.py:52
  226.8 18.1 %fusion.1 = (bf16[2,8,256,1536]{3,2,1,0:T(8,128)(2,1)}, bf16[2,8,256,1536]{3,2,1,0:T(8,128)(2,1)}) fusion(bf16[2,1,256,512]{3,2,1,0:T(8,128)(2,1)S(1)} %collective-permute-done.7, bf16[2,8,256,512]{3,2,1,0:T(8,128)(2,1)} %reshape.153, bf16[2,8,256,512]{3,2,1,0:T(8,128)(2,1)} %get-tuple-element.10, bf16[2,8,256,512]{3,2,1,0:T(8,128)(2,1)} %get-tuple-element.5, ...), kind=kLoop, calls=%fused_computation.4 | loop fusion | flops 100663296 | bytes 47185920 | tf_op jit(solution)/shard_map/concatenate | solution.py:51
  244.9 12.2 %fusion.39 = f32[4096,512]{1,0:T(8,128)} fusion(bf16[4096,1536]{1,0:T(8,128)(2,1)} %bitcast.144, bf16[1,3,1536,512]{3,2,1,0:T(8,128)(2,1)} %bitcast.176), kind=kOutput, calls=%fused_computation.71 | convolution fusion | flops 6442450944 | bytes 22544384 | tf_op jit(solution)/shard_map/dot_general | solution.py:54
  257.1 10.9 %fusion.4 = f32[4096,512]{1,0:T(8,128)} fusion(bf16[4096,512]{1,0:T(8,128)(2,1)S(1)} %bitcast.149, bf16[4096,512]{1,0:T(8,128)(2,1)} %concatenate.141, bf16[4096,512]{1,0:T(8,128)(2,1)S(1)} %bitcast.150, bf16[1,3,1536,512]{3,2,1,0:T(8,128)(2,1)} %bitcast.177), kind=kOutput, calls=%fused_computation.8 | convolution fusion | flops 6480199680 | bytes 22544384 | tf_op jit(solution)/shard_map/dot_general | solution.py:54
  268.0 14.1 %add_add_fusion = f32[4096,512]{1,0:T(8,128)S(1)} fusion(f32[4096,512]{1,0:T(8,128)} %fusion.39, f32[4096,512]{1,0:T(8,128)} %fusion.4, bf16[4096,1536]{1,0:T(8,128)(2,1)} %bitcast.143, bf16[1,3,1536,512]{3,2,1,0:T(8,128)(2,1)} %bitcast.178), kind=kOutput, calls=%fused_computation.26 | convolution fusion | flops 6446645248 | bytes 39321600 | tf_op jit(solution)/shard_map/dot_general | solution.py:54
  282.2 3.3 %add_convert_fusion = bf16[2,8,256,512]{3,2,1,0:T(8,128)(2,1)} fusion(f32[2,8,256,512]{3,2,1,0:T(8,128)S(1)} %bitcast.148, f32[512]{0:T(512)S(1)} %copy-done.42), kind=kLoop, calls=%fused_computation.25 | loop fusion | flops 4194304 | bytes 12584960 | tf_op jit(solution)/shard_map/convert_element_type | solution.py:119
  (135 shorter events, 11.7 us)
Async XLA Ops:
  0.0 4.8 %copy-start = (bf16[4096,64]{0,1:T(8,128)(2,1)S(1)}, bf16[4096,64]{0,1:T(8,128)(2,1)}, u32[]{:S(2)}) copy-start(bf16[4096,64]{0,1:T(8,128)(2,1)} %param.16) | copy-start | bytes 1572868
  0.0 3.5 %copy-start.2 = (bf16[2,4,64,4096]{3,2,1,0:T(8,128)(2,1)S(1)}, bf16[2,4,64,4096]{3,2,1,0:T(8,128)(2,1)}, u32[]{:S(2)}) copy-start(bf16[2,4,64,4096]{3,2,1,0:T(8,128)(2,1)} %param.14) | copy-start | bytes 12582916
  0.0 4.7 %copy-start.38 = (f32[2,4096]{1,0:T(2,128)S(1)}, f32[2,4096]{1,0:T(2,128)}, u32[]{:S(2)}) copy-start(f32[2,4096]{1,0:T(2,128)} %param.15) | copy-start | bytes 98308
  0.0 4.8 %copy-start.43 = (f32[64]{0:T(128)S(1)}, f32[64]{0:T(128)}, u32[]{:S(2)}) copy-start(f32[64]{0:T(128)} %param.17) | copy-start | bytes 772
  4.8 16.1 %copy-start.37 = (f32[2,4,128,16]{2,3,1,0:T(8,128)S(1)}, f32[2,4,128,16]{2,3,1,0:T(8,128)}, u32[]{:S(2)}) copy-start(f32[2,4,128,16]{2,3,1,0:T(8,128)} %param.19) | copy-start | bytes 196612
  7.5 5.9 %all-to-all-start.1 = ((f32[2,1,8192]{2,1,0:T(1,128)}), f32[2,1,8192]{2,1,0:T(1,128)S(1)}, u32[]{:S(2)}, u32[]{:S(2)}) async-start(f32[2,1,8192]{2,1,0:T(1,128)} %reshape.160), calls=%async_computation.1 | async-start | bytes 131072 | tf_op jit(solution)/shard_map/all_to_all | solution.py:104
  13.4 9.3 %all-to-all-start = ((f32[2,1,8192]{2,1,0:T(1,128)}), f32[2,1,8192]{2,1,0:T(1,128)S(1)}, u32[]{:S(2)}, u32[]{:S(2)}) async-start(f32[2,1,8192]{2,1,0:T(1,128)} %reshape.158), calls=%async_computation | async-start | bytes 131072 | tf_op jit(solution)/shard_map/all_to_all | solution.py:105
  24.0 9.0 %collective-permute-start = (bf16[2,4,128,16]{3,2,1,0:T(8,128)(2,1)S(1)}, bf16[2,4,128,16]{3,2,1,0:T(8,128)(2,1)S(1)}, u32[]{:S(2)}, u32[]{:S(2)}) collective-permute-start(bf16[2,4,128,16]{3,2,1,0:T(8,128)(2,1)S(1)} %subtract_convert_fusion), channel_id=1, source_target_pairs={{0,1},{2,3},{4,5},{6,7},{8,9},{10,11},{12,13},{14,15},{16,17},{18,... | collective-permute-start | bytes 98312 | tf_op jit(solution)/shard_map/ppermute | solution.py:12
  33.0 14.6 %copy-start.33 = (bf16[2,4,128,16]{3,2,1,0:T(8,128)(2,1)}, bf16[2,4,128,16]{3,2,1,0:T(8,128)(2,1)S(1)}, u32[]{:S(2)}) copy-start(bf16[2,4,128,16]{3,2,1,0:T(8,128)(2,1)S(1)} %collective-permute-done) | copy-start | bytes 98308
  33.2 9.7 %collective-permute-start.1 = (bf16[4,1,128,16]{2,3,1,0:T(8,128)(2,1)S(1)}, bf16[4,1,128,16]{2,3,1,0:T(8,128)(2,1)S(1)}, u32[]{:S(2)}, u32[]{:S(2)}) collective-permute-start(bf16[4,1,128,16]{2,3,1,0:T(8,128)(2,1)S(1)} %get-tuple-element.74), channel_id=1, source_target_pairs={{0,2},{2,4},{4,6},{6,8},{8,10},{10,12},{12,14},{14,16},{16,18},{18... | collective-permute-start | bytes 49160 | tf_op jit(solution)/shard_map/ppermute | solution.py:22
  39.5 8.1 %collective-permute-start.2 = (bf16[4,1,128,16]{2,3,1,0:T(8,128)(2,1)S(1)}, bf16[4,1,128,16]{2,3,1,0:T(8,128)(2,1)S(1)}, u32[]{:S(2)}, u32[]{:S(2)}) collective-permute-start(bf16[4,1,128,16]{2,3,1,0:T(8,128)(2,1)S(1)} %get-tuple-element.75), channel_id=1, source_target_pairs={{2,0},{4,2},{6,4},{8,6},{10,8},{12,10},{14,12},{16,14},{18,16},{20... | collective-permute-start | bytes 49160 | tf_op jit(solution)/shard_map/ppermute | solution.py:23
  51.1 7.2 %copy-start.24 = (bf16[2,4,128,16]{3,2,1,0:T(8,128)(2,1)S(1)}, bf16[2,4,128,16]{3,2,1,0:T(8,128)(2,1)}, u32[]{:S(2)}) copy-start(bf16[2,4,128,16]{3,2,1,0:T(8,128)(2,1)} %get-tuple-element.55) | copy-start | bytes 98308
  55.6 2.7 copy-start.28
  55.6 3.0 %copy-start.36 = (bf16[3,3,48,512]{3,2,1,0:T(8,128)(2,1)S(1)}, bf16[3,3,48,512]{3,2,1,0:T(8,128)(2,1)}, u32[]{:S(2)}) copy-start(bf16[3,3,48,512]{3,2,1,0:T(8,128)(2,1)} %param.21) | copy-start | bytes 1327108
  55.6 3.4 %copy-start.22 = (bf16[2,4,128,16]{3,2,1,0:T(8,128)(2,1)S(1)}, bf16[2,4,128,16]{3,2,1,0:T(8,128)(2,1)}, u32[]{:S(2)}) copy-start(bf16[2,4,128,16]{3,2,1,0:T(8,128)(2,1)} %get-tuple-element.58) | copy-start | bytes 98308
  55.6 3.4 %copy-start.23 = (bf16[2,4,128,16]{3,2,1,0:T(8,128)(2,1)S(1)}, bf16[2,4,128,16]{3,2,1,0:T(8,128)(2,1)}, u32[]{:S(2)}) copy-start(bf16[2,4,128,16]{3,2,1,0:T(8,128)(2,1)} %get-tuple-element.59) | copy-start | bytes 98308
  55.6 3.4 %copy-start.27 = (bf16[2,4,128,16]{3,2,1,0:T(8,128)(2,1)S(1)}, bf16[2,4,128,16]{3,2,1,0:T(8,128)(2,1)}, u32[]{:S(2)}) copy-start(bf16[2,4,128,16]{3,2,1,0:T(8,128)(2,1)} %copy.96) | copy-start | bytes 98308
  59.0 1.4 copy-start.26
  59.7 1.4 copy-start.29
  59.7 1.4 copy-start.30
  59.7 1.4 copy-start.31
  59.7 1.4 copy-start.32
  59.7 1.4 copy-start.34
  59.7 1.4 copy-start.35
  60.6 1.4 copy-start.25
  62.0 1.3 copy-start.39
  63.4 1.8 copy-start.40
  65.8 24.4 %collective-permute-start.3 = (bf16[2,4,128,512]{3,2,1,0:T(8,128)(2,1)S(1)}, bf16[2,4,128,512]{3,2,1,0:T(8,128)(2,1)S(1)}, u32[]{:S(2)}, u32[]{:S(2)}) collective-permute-start(bf16[2,4,128,512]{3,2,1,0:T(8,128)(2,1)S(1)} %fusion.36), channel_id=1, source_target_pairs={{0,1},{2,3},{4,5},{6,7},{8,9},{10,11},{12,13},{14,15},{16,17},{18,... | collective-permute-start | bytes 3145736 | tf_op jit(solution)/shard_map/ppermute | solution.py:12
  90.4 15.3 %collective-permute-start.4 = (bf16[4,1,128,512]{3,2,1,0:T(8,128)(2,1)S(1)}, bf16[4,1,128,512]{3,2,1,0:T(8,128)(2,1)S(1)}, u32[]{:S(2)}, u32[]{:S(2)}) collective-permute-start(bf16[4,1,128,512]{3,2,1,0:T(8,128)(2,1)S(1)} %get-tuple-element.41), channel_id=1, source_target_pairs={{0,2},{2,4},{4,6},{6,8},{8,10},{10,12},{12,14},{14,16},{16,18},{18... | collective-permute-start | bytes 1572872 | tf_op jit(solution)/shard_map/ppermute | solution.py:22
  94.7 13.5 %collective-permute-start.5 = (bf16[4,1,128,512]{3,2,1,0:T(8,128)(2,1)S(1)}, bf16[4,1,128,512]{3,2,1,0:T(8,128)(2,1)S(1)}, u32[]{:S(2)}, u32[]{:S(2)}) collective-permute-start(bf16[4,1,128,512]{3,2,1,0:T(8,128)(2,1)S(1)} %get-tuple-element.42), channel_id=1, source_target_pairs={{2,0},{4,2},{6,4},{8,6},{10,8},{12,10},{14,12},{16,14},{18,16},{20... | collective-permute-start | bytes 1572872 | tf_op jit(solution)/shard_map/ppermute | solution.py:23
  124.0 4.7 %copy-start.10 = (bf16[2,4,128,512]{3,2,1,0:T(8,128)(2,1)S(1)}, bf16[2,4,128,512]{3,2,1,0:T(8,128)(2,1)}, u32[]{:S(2)}) copy-start(bf16[2,4,128,512]{3,2,1,0:T(8,128)(2,1)} %get-tuple-element.20) | copy-start | bytes 3145732
  124.0 4.7 %copy-start.11 = (bf16[2,4,128,512]{3,2,1,0:T(8,128)(2,1)S(1)}, bf16[2,4,128,512]{3,2,1,0:T(8,128)(2,1)}, u32[]{:S(2)}) copy-start(bf16[2,4,128,512]{3,2,1,0:T(8,128)(2,1)} %get-tuple-element.21) | copy-start | bytes 3145732
  124.0 4.7 %copy-start.15 = (bf16[2,4,128,512]{3,2,1,0:T(8,128)(2,1)S(1)}, bf16[2,4,128,512]{3,2,1,0:T(8,128)(2,1)}, u32[]{:S(2)}) copy-start(bf16[2,4,128,512]{3,2,1,0:T(8,128)(2,1)} %get-tuple-element.34) | copy-start | bytes 3145732
  129.1 4.7 %copy-start.8 = (bf16[2,4,128,512]{3,2,1,0:T(8,128)(2,1)S(1)}, bf16[2,4,128,512]{3,2,1,0:T(8,128)(2,1)}, u32[]{:S(2)}) copy-start(bf16[2,4,128,512]{3,2,1,0:T(8,128)(2,1)} %get-tuple-element.24) | copy-start | bytes 3145732
  129.1 4.7 %copy-start.9 = (bf16[2,4,128,512]{3,2,1,0:T(8,128)(2,1)S(1)}, bf16[2,4,128,512]{3,2,1,0:T(8,128)(2,1)}, u32[]{:S(2)}) copy-start(bf16[2,4,128,512]{3,2,1,0:T(8,128)(2,1)} %get-tuple-element.25) | copy-start | bytes 3145732
  129.1 4.7 %copy-start.16 = (bf16[2,4,128,512]{3,2,1,0:T(8,128)(2,1)S(1)}, bf16[2,4,128,512]{3,2,1,0:T(8,128)(2,1)}, u32[]{:S(2)}) copy-start(bf16[2,4,128,512]{3,2,1,0:T(8,128)(2,1)} %get-tuple-element.38) | copy-start | bytes 3145732
  134.1 4.7 %copy-start.6 = (bf16[2,4,128,512]{3,2,1,0:T(8,128)(2,1)S(1)}, bf16[2,4,128,512]{3,2,1,0:T(8,128)(2,1)}, u32[]{:S(2)}) copy-start(bf16[2,4,128,512]{3,2,1,0:T(8,128)(2,1)} %get-tuple-element.26) | copy-start | bytes 3145732
  134.1 4.7 %copy-start.7 = (bf16[2,4,128,512]{3,2,1,0:T(8,128)(2,1)S(1)}, bf16[2,4,128,512]{3,2,1,0:T(8,128)(2,1)}, u32[]{:S(2)}) copy-start(bf16[2,4,128,512]{3,2,1,0:T(8,128)(2,1)} %get-tuple-element.27) | copy-start | bytes 3145732
  134.1 4.7 %copy-start.13 = (bf16[2,4,128,512]{3,2,1,0:T(8,128)(2,1)S(1)}, bf16[2,4,128,512]{3,2,1,0:T(8,128)(2,1)}, u32[]{:S(2)}) copy-start(bf16[2,4,128,512]{3,2,1,0:T(8,128)(2,1)} %get-tuple-element.35) | copy-start | bytes 3145732
  139.1 4.7 %copy-start.5 = (bf16[2,4,128,512]{3,2,1,0:T(8,128)(2,1)S(1)}, bf16[2,4,128,512]{3,2,1,0:T(8,128)(2,1)}, u32[]{:S(2)}) copy-start(bf16[2,4,128,512]{3,2,1,0:T(8,128)(2,1)} %get-tuple-element.31) | copy-start | bytes 3145732
  139.1 4.7 %copy-start.14 = (bf16[2,4,128,512]{3,2,1,0:T(8,128)(2,1)S(1)}, bf16[2,4,128,512]{3,2,1,0:T(8,128)(2,1)}, u32[]{:S(2)}) copy-start(bf16[2,4,128,512]{3,2,1,0:T(8,128)(2,1)} %get-tuple-element.36) | copy-start | bytes 3145732
  157.4 4.7 %copy-start.12 = (bf16[2,4,128,512]{3,2,1,0:T(8,128)(2,1)S(1)}, bf16[2,4,128,512]{3,2,1,0:T(8,128)(2,1)}, u32[]{:S(2)}) copy-start(bf16[2,4,128,512]{3,2,1,0:T(8,128)(2,1)} %get-tuple-element.33) | copy-start | bytes 3145732
  157.4 5.2 %copy-start.20 = (f32[1024,512]{1,0:T(8,128)S(1)}, f32[1024,512]{1,0:T(8,128)}, u32[]{:S(2)}) copy-start(f32[1024,512]{1,0:T(8,128)} %fusion.52) | copy-start | bytes 6291460
  157.4 5.2 %copy-start.21 = (f32[1024,512]{1,0:T(8,128)S(1)}, f32[1024,512]{1,0:T(8,128)}, u32[]{:S(2)}) copy-start(f32[1024,512]{1,0:T(8,128)} %fusion.56) | copy-start | bytes 6291460
  162.0 1.6 copy-start.17
  162.0 2.2 copy-start.18
  162.0 2.9 copy-start.19
  164.9 5.3 %copy-start.41 = (f32[512]{0:T(512)S(1)}, f32[512]{0:T(512)}, u32[]{:S(2)}) copy-start(f32[512]{0:T(512)} %param.25) | copy-start | bytes 6148
  183.0 19.1 %collective-permute-start.7 = (bf16[2,1,256,512]{3,2,1,0:T(8,128)(2,1)S(1)}, bf16[2,1,256,512]{3,2,1,0:T(8,128)(2,1)S(1)}, u32[]{:S(2)}, u32[]{:S(2)}) collective-permute-start(bf16[2,1,256,512]{3,2,1,0:T(8,128)(2,1)S(1)} %get-tuple-element.13), channel_id=1, source_target_pairs={{2,0},{4,2},{6,4},{8,6},{10,8},{12,10},{14,12},{16,14},{18,16},{20... | collective-permute-start | bytes 1572872 | tf_op jit(solution)/shard_map/ppermute | solution.py:23
  184.9 17.2 %collective-permute-start.6 = (bf16[2,1,256,512]{3,2,1,0:T(8,128)(2,1)S(1)}, bf16[2,1,256,512]{3,2,1,0:T(8,128)(2,1)S(1)}, u32[]{:S(2)}, u32[]{:S(2)}) collective-permute-start(bf16[2,1,256,512]{3,2,1,0:T(8,128)(2,1)S(1)} %get-tuple-element.14), channel_id=1, source_target_pairs={{0,2},{2,4},{4,6},{6,8},{8,10},{10,12},{12,14},{14,16},{16,18},{18... | collective-permute-start | bytes 1572872 | tf_op jit(solution)/shard_map/ppermute | solution.py:22
  244.9 12.2 %copy-start.3 = (bf16[2,8,256,512]{3,2,1,0:T(8,128)(2,1)S(1)}, bf16[2,8,256,512]{3,2,1,0:T(8,128)(2,1)}, u32[]{:S(2)}) copy-start(bf16[2,8,256,512]{3,2,1,0:T(8,128)(2,1)} %get-tuple-element.6) | copy-start | bytes 12582916
  244.9 12.2 %copy-start.4 = (bf16[2,8,256,512]{3,2,1,0:T(8,128)(2,1)S(1)}, bf16[2,8,256,512]{3,2,1,0:T(8,128)(2,1)}, u32[]{:S(2)}) copy-start(bf16[2,8,256,512]{3,2,1,0:T(8,128)(2,1)} %get-tuple-element.7) | copy-start | bytes 12582916
  268.0 14.1 %copy-start.42 = (f32[512]{0:T(512)S(1)}, f32[512]{0:T(512)}, u32[]{:S(2)}) copy-start(f32[512]{0:T(512)} %param.27) | copy-start | bytes 6148
  282.1 3.3 %copy-start.1 = (bf16[4096,64]{0,1:T(8,128)(2,1)S(1)}, bf16[4096,64]{0,1:T(8,128)(2,1)}, u32[]{:S(2)}) copy-start(bf16[4096,64]{0,1:T(8,128)(2,1)} %param.16) | copy-start | bytes 1572868
where the time goes:
time: 291 us; the launch traced here: 286 us
  matrix products  85.8 us (29%)
  local copies, waits for them, and re-layouts  63.1 us (22%)
  waiting for transfers between devices  50.9 us (17%)
  other arithmetic  46.4 us (16%)
  starting transfers between devices  37.1 us (13%)
    dot_general x21, matrix products, apply_taps(): jnp.dot(window.reshape(-1, 3 * channels), weight[step_t, step_h], preferr...  84 us
    slice x14, local copies, waits for them, and re-layouts, apply_taps(): block_slice[:, :, step_w:step_w + col_count]  37 us
    ppermute x2, waiting for transfers between devices, shifted(): return lax.ppermute(x, axis, pairs)  30.7 us
    concatenate x16, other arithmetic, apply_taps(): jnp.concatenate([block_slice[:, :, step_w:step_w + col_count] for step_w...  26.1 us
    ppermute x3, starting transfers between devices, padded_2(): before = lax.ppermute(last, axis, up)  17.4 us
    ppermute x3, waiting for transfers between devices, padded_2(): after = lax.ppermute(first, axis, down)  10.6 us
    concatenate x5, other arithmetic, padded_2(): x = jnp.concatenate([before, x, after], axis=dim)  9.86 us
    ppermute x3, waiting for transfers between devices, padded_2(): before = lax.ppermute(last, axis, up)  8.82 us
  transfers between devices with their start and end apart: 10, of which 7 were waited for; matrix products, arithmetic and copies ran while one was open for 4% of the time, Pallas kernels for 0%

commit v1 on v0

v1 whole, which is shorter than its diff:
```python
import functools

import jax
import jax.numpy as jnp
from jax import lax
from jax.experimental import pallas as pl
from jax.experimental.pallas import tpu as pltpu
from jax.sharding import PartitionSpec as P

MESH = pl.DeviceIdType.MESH
norm_eps = 1e-06
bf16, f32 = jnp.bfloat16, jnp.float32
CH = 512
Q = 64


def moved_down(x):
    at = lax.broadcasted_iota(jnp.int32, x.shape, 0)
    return jnp.where(at == 0, 0.0, pltpu.roll(x, 1, 0))


def moved_up(x):
    at = lax.broadcasted_iota(jnp.int32, x.shape, 0)
    return jnp.where(at == x.shape[0] - 1, 0.0, pltpu.roll(x, x.shape[0] - 1, 0))


def latent_kernel(
    h_ref, mod_ref, w_ref, b_ref, g_ref, sigma_ref, x_ref, land,
    hbuf, wbuf, mod, wmat, bias_in, scalars, xall, xt, lat, hsem, ssmall, xlocal, xsend, xrecv, ssem, rsem,
):
    s, t = lax.axis_index("space"), lax.axis_index("tm")
    ns = lax.axis_size("space")
    other = 1 - t
    after, before = lax.rem(s + 1, ns), lax.rem(s + ns - 1, ns)

    small = []
    for n, (a, b) in enumerate(
        ((w_ref, wbuf), (mod_ref, mod), (b_ref, bias_in), (g_ref, scalars.at[0]), (sigma_ref, scalars.at[1]))
    ):
        load = pltpu.make_async_copy(a, b, ssmall.at[n])
        load.start()
        small.append(load)
    loads = []
    for f in range(4):
        load = pltpu.make_async_copy(h_ref.at[:, f], hbuf.at[f], hsem.at[f])
        load.start()
        loads.append(load)
    x_load = pltpu.make_async_copy(x_ref, xall.at[t], xlocal)
    x_load.start()

    land[...] = jnp.zeros(land.shape, bf16)
    peers = [(s, other), (after, 0), (after, 1), (before, 0), (before, 1)]
    barrier = pltpu.get_barrier_semaphore()
    for peer in peers:
        pl.semaphore_signal(barrier, inc=1, device_id=peer, device_id_type=MESH)

    for load in small:
        load.wait()
    scale = 1.0 + mod[1:2, :]
    shift = mod[0:1, :]
    wide = wbuf[...].astype(f32)
    ordered = jnp.concatenate(
        [wide[block * 16 : block * 16 + 16] for block in (0, 2, 1, 3)], axis=0
    )
    both = jnp.concatenate([ordered * scale, ordered], axis=0)
    for k in range(8):
        at = slice(k * 512, (k + 1) * 512)
        wmat[at] = jnp.transpose(both[:, at]).astype(bf16)
    shift_hi = shift.astype(bf16)
    shift_lo = (shift - shift_hi.astype(f32)).astype(bf16)
    row = lax.broadcasted_iota(jnp.int32, (16, shift.shape[1]), 0)
    sums = jnp.where(
        row == 0,
        1.0,
        jnp.where(
            row == 1, shift_hi.astype(f32), jnp.where(row == 2, shift_lo.astype(f32), 0.0)
        ),
    ).astype(bf16)
    lane = lax.broadcasted_iota(jnp.int32, (Q, Q), 1)
    source = ((lane // 16) % 2) * 32 + (lane // 32) * 16 + lane % 16
    one_hot = (lax.broadcasted_iota(jnp.int32, (Q, Q), 0) == source).astype(f32)
    bias = jnp.dot(
        jnp.broadcast_to(bias_in[...], (8, Q)), one_hot,
        preferred_element_type=f32, precision=lax.Precision.HIGHEST,
    )[0:1]

    totals = jnp.dot(sums, wmat[...], preferred_element_type=f32)
    column_sum = totals[0:1, :Q]
    constant = totals[1:2, Q:] + totals[2:3, Q:] + bias

    pl.semaphore_wait(barrier, 5)
    x_copy = pltpu.make_async_remote_copy(
        src_ref=x_ref, dst_ref=xall.at[t], send_sem=xsend, recv_sem=xrecv,
        device_id=(s, other), device_id_type=MESH,
    )
    x_copy.start()

    guidance, sigma = scalars[0], scalars[1]
    predictions = []
    for pair in range(2):
        loads[2 * pair].wait()
        loads[2 * pair + 1].wait()
        product = jnp.dot(
            hbuf[2 * pair : 2 * pair + 2].reshape(4 * Q, 4096), wmat[...],
            preferred_element_type=f32,
        )
        for f in range(2):
            rows = hbuf[2 * pair + f].reshape(2 * Q, 4096)
            pivot = rows[:, 0:1].astype(f32)
            first, second = jnp.zeros((2 * Q, 128), f32), jnp.zeros((2 * Q, 128), f32)
            for k in range(32):
                part = rows[:, k * 128 : (k + 1) * 128].astype(f32) - pivot
                first = first + part
                second = second + part * part
            offset = jnp.sum(first, axis=1, keepdims=True) * (1.0 / 4096)
            spread = jnp.sum(second, axis=1, keepdims=True) * (1.0 / 4096) - offset * offset
            inverse = lax.rsqrt(jnp.maximum(spread, 0.0) + norm_eps)
            own = product[2 * f * Q : 2 * (f + 1) * Q, :Q]
            branch = inverse * (own - (pivot + offset) * column_sum)
            cond, uncond = branch[:Q], branch[Q:]
            predictions.append(uncond + guidance * (cond - uncond) + constant)

    x_load.wait()
    x_copy.wait()
    xt[...] = jnp.transpose(
        jnp.concatenate([xall[f // 2, f % 2, 2 * t + a] for f in range(4) for a in range(2)], axis=0)
    )
    even, odd = xt[pl.ds(0, Q, stride=2), :], xt[pl.ds(1, Q, stride=2), :]
    position = lax.broadcasted_iota(jnp.int32, (Q, Q), 0)
    compact = []
    for f in range(4):
        at = slice(32 * f, 32 * f + 32)
        noisy = jnp.concatenate([even[:, at], odd[:, at]], axis=1)
        latent = noisy - sigma * predictions[f]
        from_left = jnp.where(position == 0, 0.0, pltpu.roll(latent, 1, 0))
        from_right = jnp.where(position == Q - 1, 0.0, pltpu.roll(latent, Q - 1, 0))
        beside = jnp.where(lane < 32, from_right, from_left)
        compact.append(jnp.concatenate([latent, beside], axis=1).astype(bf16))
    to = lax.broadcasted_iota(jnp.int32, (128, 128), 1)
    source = ((to // 16 + 3) % 4) * 32 + (to // 64) * 16 + to % 16
    widen = (lax.broadcasted_iota(jnp.int32, (128, 128), 0) == source).astype(f32).astype(bf16)
    lat[...] = jnp.dot(
        jnp.concatenate(compact, axis=0), widen, preferred_element_type=f32
    ).astype(bf16).reshape(4, Q, 128)

    def send(peer, to, slot, k):
        count = 2 + 2 * to
        return pltpu.make_async_remote_copy(
            src_ref=lat.at[pl.ds(0, count)], dst_ref=land.at[slot, pl.ds(6 - count, count)],
            send_sem=ssem.at[k], recv_sem=rsem.at[slot], device_id=peer, device_id_type=MESH,
        )

    sends = [
        send((before, 1), 1, 4 + t, 0), send((after, 1), 1, t, 1),
        send((before, 0), 0, 4 + t, 2), send((after, 0), 0, t, 3),
    ]
    for to in range(2):
        @pl.when(other == to)
        def _():
            send((s, to), to, 3 - to, 4).start()
    for copy in sends:
        copy.start()

    for me in range(2):
        @pl.when(t == me)
        def _():
            count = 2 + 2 * me
            land[2 + me, 6 - count : 6] = lat[0:count]
            for slot in (3 - me, 0, 1, 4, 5):
                send((s, other), me, slot, 4).wait_recv()
            send((s, other), 1 - me, 2 + me, 4).wait_send()
    for copy in sends:
        copy.wait_send()

    @pl.when(s == 0)
    def _():
        land[0:2] = jnp.zeros((2, 6, Q, 128), bf16)

    @pl.when(s == ns - 1)
    def _():
        land[4:6] = jnp.zeros((2, 6, Q, 128), bf16)


def decoder_kernel(
    lat_ref, win_ref, bin_ref, gain_ref, wmid_ref, bmid_ref, wup_ref, bup_ref, out_ref,
    land, win, vectors, wm, wu, wp, windows, comps, skip, staged, mixed, pending, fine,
    wrow, wphase, spread, phases, lsem, wsem, vsem, msem, usem, osem,
):
    s, t = lax.axis_index("space"), lax.axis_index("tm")
    ns = lax.axis_size("space")
    lat_load = pltpu.make_async_copy(lat_ref, land, lsem)
    lat_load.start()
    others = [pltpu.make_async_copy(win_ref, win, wsem)]
    for n, ref in enumerate((bin_ref, gain_ref, bmid_ref, bup_ref)):
        others.append(pltpu.make_async_copy(ref, vectors.at[n], vsem.at[n]))
    mids = [pltpu.make_async_copy(wmid_ref.at[i], wm.at[i], msem.at[i]) for i in range(3)]
    up_load = pltpu.make_async_copy(wup_ref, wu, usem)
    for load in others + mids + [up_load]:
        load.start()

    wp[...] = jnp.zeros(wp.shape, bf16)
    to = lax.broadcasted_iota(jnp.int32, (256, 256), 0)
    at = lax.broadcasted_iota(jnp.int32, (256, 256), 1)
    spread[...] = jnp.where(
        to == 4 * (at % 64) + 2 * ((at // 64) % 2) + at // 128, 1.0, 0.0
    ).astype(bf16)
    for load in others:
        load.wait()
    for i in range(3):
        for j in range(3):
            block = win[i, j]
            for a in range(2):
                for b in range(2):
                    at = i * 256 + ((a + j - 1) % 4) * 64 + b * 16
                    wp[at : at + 48, (2 * a + b) * CH : (2 * a + b + 1) * CH] = block
    lat_load.wait()
    lane = lax.broadcasted_iota(jnp.int32, (Q, 128), 1)
    for p in range(4):
        for f in range(6):
            beside = jnp.where(
                lane < 64, land[p + 2, f].astype(f32), land[p, f].astype(f32)
            ).astype(bf16)
            windows[p, f] = jnp.concatenate([land[p + 1, f], beside], axis=1)

    bias_first, half_gain = vectors[0], 0.5 * vectors[1]
    bias_mid, bias_up = vectors[2], vectors[3]
    frame = lax.broadcasted_iota(jnp.int32, (4 * Q, 1), 0) // Q
    frame_held = jnp.logical_or(frame >= 2, t > 0)

    def patch_row(p, _):
        lhs = jnp.concatenate(
            [windows[p, i : i + 4].reshape(4 * Q, 256) for i in range(3)], axis=1
        )
        for a in range(2):
            line = 2 * p + a
            held = jnp.logical_and(4 * s - 2 + line >= 0, 4 * s - 2 + line < 4 * ns)
            mask = jnp.where(jnp.logical_and(frame_held, held), 1.0, 0.0)
            sides = []
            for b in range(2):
                column = (2 * a + b) * CH
                value = jnp.dot(
                    lhs, wp[:, column : column + CH], preferred_element_type=f32
                ) + bias_first
                for f in range(2):
                    skip[f, b, line] = value[(2 + f) * Q : (3 + f) * Q].astype(bf16)
                power = jnp.mean(value * value, axis=1, keepdims=True)
                half = value * (lax.rsqrt(power + norm_eps) * mask) * half_gain
                active = half * jnp.tanh(half) + half
                a0, a1, a2, a3 = [active[f * Q : (f + 1) * Q] for f in range(4)]
                sides.append((a0 - a2, a1 + a2, a2 - a1, a1 - a3))
            for k in range(4):
                even, odd = sides[0][k], sides[1][k]
                comps[4 * k, line] = (moved_down(odd) - odd).astype(bf16)
                comps[4 * k + 1, line] = (even + odd).astype(bf16)
                comps[4 * k + 2, line] = (odd - even).astype(bf16)
                comps[4 * k + 3, line] = (even - moved_up(even)).astype(bf16)
        return 0

    lax.fori_loop(0, 4, patch_row, 0)

    def finish(f, b, n, middle):
        cols = slice(n * 256, (n + 1) * 256)
        for r in range(6):
            line = 4 * s - 1 + r
            held = jnp.where(jnp.logical_and(line >= 0, line < 4 * ns), 1.0, 0.0)
            value = (
                skip[f, b, r + 1, :, cols].astype(f32)
                + middle[r * Q : (r + 1) * Q]
                + bias_mid[:, cols]
            ) * held
            fine[f, r, 1 + b, :, cols] = value.astype(bf16)
            if b == 0:
                fine[f, r, 3, :, cols] = moved_up(value).astype(bf16)
            else:
                fine[f, r, 0, :, cols] = moved_down(value).astype(bf16)

    def phase_weights(a):
        both = (wu.at[1], wu.at[2]) if a == 0 else (wu.at[0], wu.at[1])
        alone = wu.at[2 * a]
        wrow[...] = both[0][...] + both[1][...]
        for i in range(2):
            held = alone if i == a else wrow
            k0, k1, k2 = [held[k * CH : (k + 1) * CH] for k in range(3)]
            for n, value in enumerate((k0, k1 + k2, k0 + k1, k2)):
                wphase[a, i, n] = value

    for k in range(4):
        if k == 0:
            mids[0].wait()
        if k == 1:
            mids[1].wait()
            mids[2].wait()
            up_load.wait()
        if k > 1:
            phase_weights(k - 2)
        source = wm.at[0] if k == 0 else wm.at[2] if k == 3 else staged
        if k in (1, 2):
            for j in range(3):
                ends = wm[0, j] + wm[2, j]
                staged[j] = ends + wm[1, j] if k == 1 else ends - wm[1, j]
        for j in range(3):
            left, centre, right = [source[j, c * CH : (c + 1) * CH] for c in range(3)]
            mixed[0, j * CH : (j + 1) * CH] = left + right + centre
            mixed[1, j * CH : (j + 1) * CH] = left + right - centre
        for n in range(2):
            cols = slice(n * 256, (n + 1) * 256)
            products = []
            for c in range(4):
                lhs = jnp.concatenate(
                    [comps[4 * k + c, j : j + 6].reshape(6 * Q, CH) for j in range(3)], axis=1
                )
                if c in (1, 2):
                    rhs = mixed[c - 1, :, cols]
                else:
                    at = 0 if c == 0 else 2 * CH
                    rhs = jnp.concatenate(
                        [source[j, at : at + CH, cols] for j in range(3)], axis=0
                    )
                products.append(jnp.dot(lhs, rhs, preferred_element_type=f32))
            m0, m1, m2, m3 = products
            for b, total in enumerate((m0 + 0.5 * (m1 + m2), 0.5 * (m1 - m2) - m3)):
                if k == 0:
                    pending[0, b, :, cols] = total
                elif k == 1:
                    pending[1, b, :, cols] = total
                elif k == 2:
                    held = pending[1, b, :, cols]
                    pending[1, b, :, cols] = 0.5 * (held - total)
                    finish(0, b, n, pending[0, b, :, cols] + 0.5 * (held + total))
                else:
                    finish(1, b, n, pending[1, b, :, cols] - total)

    writes = []

    def order_lines(f, a):
        lines = jnp.dot(
            spread[...],
            jnp.concatenate([phases[f, r].reshape(256, CH) for r in range(4)], axis=1),
            preferred_element_type=f32,
        ).astype(bf16)
        base = 8 * a + 4 * f
        for r in range(4):
            comps[base + r, 0:4] = lines[:, r * CH : (r + 1) * CH].reshape(4, Q, CH)
        write = pltpu.make_async_copy(
            comps.at[base : base + 4, 0:4], out_ref.at[f, :, a], osem.at[2 * a + f]
        )
        write.start()
        writes.append(write)

    behind = None
    for a in range(2):
        for f in range(2):
            for n in range(2):
                cols = slice(n * 256, (n + 1) * 256)
                for b in range(2):
                    lhs = jnp.concatenate(
                        [
                            fine[f, a + i : a + i + 4, b + c : b + c + 2].reshape(8 * Q, CH)
                            for i in range(2)
                            for c in range(2)
                        ],
                        axis=1,
                    )
                    rhs = wphase[a, :, 2 * b : 2 * b + 2, :, cols].reshape(4 * CH, 256)
                    value = jnp.dot(lhs, rhs, preferred_element_type=f32) + bias_up[:, cols]
                    phases[f, :, b, :, cols] = value.astype(bf16).reshape(4, 2 * Q, 256)
            if behind is not None:
                order_lines(*behind)
            behind = (f, a)
    order_lines(*behind)
    for write in writes:
        write.wait()


def on_device(
    hidden, modulation, w_proj, b_proj, guidance, x_noisy, sigma, w_in, b_in, gain,
    w_mid, b_mid, w_up, b_up,
):
    vmem = pl.BlockSpec(memory_space=pltpu.VMEM)
    anywhere = pl.BlockSpec(memory_space=pltpu.HBM)
    rows = lambda v: v.reshape(1, -1)
    dma = pltpu.SemaphoreType.DMA
    latents = pl.pallas_call(
        latent_kernel,
        out_shape=jax.ShapeDtypeStruct((6, 6, Q, 128), bf16),
        in_specs=[anywhere] * 7,
        out_specs=vmem,
        scratch_shapes=[
            pltpu.VMEM((4, 2, Q, 4096), bf16),
            pltpu.VMEM((64, 4096), bf16),
            pltpu.VMEM((2, 4096), f32),
            pltpu.VMEM((4096, 128), bf16),
            pltpu.VMEM((1, 64), f32),
            pltpu.VMEM((2, 1, 1), f32),
            pltpu.VMEM((2, 2, 4, 16, 128), f32),
            pltpu.VMEM((128, 128), f32),
            pltpu.VMEM((4, Q, 128), bf16),
            dma((4,)), dma((5,)), dma, dma, dma, dma((5,)), dma((6,)),
        ],
        compiler_params=pltpu.CompilerParams(
            collective_id=0, has_side_effects=True, vmem_limit_bytes=60 << 20
        ),
    )(
        hidden, modulation, w_proj.T, rows(b_proj), rows(guidance), rows(sigma),
        jnp.swapaxes(x_noisy, 2, 3),
    )
    decoded = pl.pallas_call(
        decoder_kernel,
        out_shape=jax.ShapeDtypeStruct((2, 4, 2, 4, Q, CH), bf16),
        in_specs=[anywhere] * 8,
        out_specs=anywhere,
        scratch_shapes=[
            pltpu.VMEM((6, 6, Q, 128), bf16),
            pltpu.VMEM((3, 3, 48, CH), bf16),
            pltpu.VMEM((4, 1, CH), f32),
            pltpu.VMEM((3, 3, 3 * CH, CH), bf16),
            pltpu.VMEM((3, 3 * CH, CH), bf16),
            pltpu.VMEM((768, 4 * CH), bf16),
            pltpu.VMEM((4, 6, Q, 256), bf16),
            pltpu.VMEM((16, 8, Q, CH), bf16),
            pltpu.VMEM((2, 2, 8, Q, CH), bf16),
            pltpu.VMEM((3, 3 * CH, CH), bf16),
            pltpu.VMEM((2, 3 * CH, CH), bf16),
            pltpu.VMEM((2, 2, 6 * Q, CH), f32),
            pltpu.VMEM((2, 6, 4, Q, CH), bf16),
            pltpu.VMEM((3 * CH, CH), bf16),
            pltpu.VMEM((2, 2, 4, CH, CH), bf16),
            pltpu.VMEM((256, 256), bf16),
            pltpu.VMEM((2, 4, 2, 2 * Q, CH), bf16),
            dma, dma, dma((4,)), dma((3,)), dma, dma((4,)),
        ],
        compiler_params=pltpu.CompilerParams(vmem_limit_bytes=62 << 20),
    )(latents, w_in, rows(b_in), rows(gain), w_mid, rows(b_mid), w_up, rows(b_up))
    return decoded.reshape(2, 8, 256, CH)


def solution(mesh):
    return jax.shard_map(
        on_device,
        mesh=mesh,
        in_specs=(
            P(None, None, ("space", "tm"), None), P(), P(), P(), P(),
            P("tm", "space", None, None), P(), P(), P(), P(), P(), P(), P(), P(),
        ),
        out_specs=P("tm", "space", None, None),
        check_vma=False,
    )
```

time: 291 us -> 54.6 us (0.19)
  the two profiles are of different devices: /device:TPU:31 before, /device:TPU:1 now
where the time goes in v1:
time: 54.6 us; the launch traced here: 54.5 us
  Pallas kernels  53 us (97%)
  between operations  1.49 us (3%)
    pallas_call x1, Pallas kernels, on_device(): pl.pallas_call(decoder_kernel, out_shape=jax.ShapeDtypeStruct((2, 4, 2, 4...  33.5 us
    pallas_call x1, Pallas kernels, on_device(): pl.pallas_call(latent_kernel, out_shape=jax.ShapeDtypeStruct((6, 6, Q, 12...  19.6 us

profile of v1, /device:TPU:1, one launch (start us, length us, event | category | flops | bytes accessed | tf_op | source)
XLA Modules:
  0.0 54.5 jit_solution(8771889848158657623)
XLA Ops:
  1.3 19.6 %shard_map.136.lat_ref = bf16[6,6,64,128]{3,2,1,0:T(8,128)(2,1)} custom-call(bf16[2,4,64,4096]{3,2,1,0:T(8,128)(2,1)} %h_ref.1, f32[2,4096]{1,0:T(2,128)} %mod_ref.1, bf16[64,4096]{1,0:T(8,128)(2,1)} %bitcast.12, f32[1,64]{1,0:T(1,128)} %bitcast.18, f32[1,1]{1,0:T(1,128)} %bitcast.10.g_ref, f32[1,1]{1,0:T(1,128)} %bitcast.11.sigma_ref, ...), custom_call_target="tpu_custom_call" | custom-call | tf_op jit(solution)/shard_map/pallas_call | solution.py:383
  20.9 33.5 %shard_map.137 = bf16[2,4,2,4,64,512]{5,4,3,2,1,0:T(8,128)(2,1)} custom-call(bf16[6,6,64,128]{3,2,1,0:T(8,128)(2,1)} %shard_map.136.lat_ref, bf16[3,3,48,512]{3,2,1,0:T(8,128)(2,1)} %win_ref.1, f32[1,512]{1,0:T(1,128)} %bitcast.14, f32[1,512]{1,0:T(1,128)} %bitcast.15, bf16[3,3,1536,512]{3,2,1,0:T(8,128)(2,1)} %wmid_ref.1, f32[1,512]{1,0:T(1,128)} %bitcast.16, ...), custom_call_target="tpu_custom_call" | custom-call | tf_op jit(solution)/shard_map/pallas_call | solution.py:407

commit v2 on v1

--- a/solution.py
+++ b/solution.py
@@ -25,13 +25,14 @@
 
 
 def latent_kernel(
-    h_ref, mod_ref, w_ref, b_ref, g_ref, sigma_ref, x_ref, land,
-    hbuf, wbuf, mod, wmat, bias_in, scalars, xall, xt, lat, hsem, ssmall, xlocal, xsend, xrecv, ssem, rsem,
+    h_ref, mod_ref, w_ref, b_ref, g_ref, sigma_ref, x_ref, windows,
+    hbuf, wbuf, mod, wmat, bias_in, scalars, xall, xt, lat, land,
+    hsem, ssmall, xlocal, xsend, xrecv, ssem, rsem,
 ):
     s, t = lax.axis_index("space"), lax.axis_index("tm")
     ns = lax.axis_size("space")
     other = 1 - t
-    after, before = lax.rem(s + 1, ns), lax.rem(s + ns - 1, ns)
+    after, before = s + 1, s - 1
 
     small = []
     for n, (a, b) in enumerate(
@@ -49,10 +50,13 @@
     x_load.start()
 
     land[...] = jnp.zeros(land.shape, bf16)
-    peers = [(s, other), (after, 0), (after, 1), (before, 0), (before, 1)]
     barrier = pltpu.get_barrier_semaphore()
-    for peer in peers:
-        pl.semaphore_signal(barrier, inc=1, device_id=peer, device_id_type=MESH)
+    pl.semaphore_signal(barrier, inc=1, device_id=(s, other), device_id_type=MESH)
+    for held, row in ((s > 0, before), (s < ns - 1, after)):
+        @pl.when(held)
+        def _():
+            for k in range(2):
+                pl.semaphore_signal(barrier, inc=1, device_id=(row, k), device_id_type=MESH)
 
     for load in small:
         load.wait()
@@ -88,7 +92,9 @@
     column_sum = totals[0:1, :Q]
     constant = totals[1:2, Q:] + totals[2:3, Q:] + bias
 
-    pl.semaphore_wait(barrier, 5)
+    pl.semaphore_wait(
+        barrier, 1 + 2 * (s > 0).astype(jnp.int32) + 2 * (s < ns - 1).astype(jnp.int32)
+    )
     x_copy = pltpu.make_async_remote_copy(
         src_ref=x_ref, dst_ref=xall.at[t], send_sem=xsend, recv_sem=xrecv,
         device_id=(s, other), device_id_type=MESH,
@@ -150,62 +156,75 @@
             send_sem=ssem.at[k], recv_sem=rsem.at[slot], device_id=peer, device_id_type=MESH,
         )
 
-    sends = [
-        send((before, 1), 1, 4 + t, 0), send((after, 1), 1, t, 1),
-        send((before, 0), 0, 4 + t, 2), send((after, 0), 0, t, 3),
-    ]
+    def send_row(row, slot, k):
+        return [send((row, 1), 1, slot, k), send((row, 0), 0, slot, k + 1)]
+
+    rows_held = ((s > 0, before, 4 + t, 0), (s < ns - 1, after, t, 2))
+    for held, row, slot, k in rows_held:
+        @pl.when(held)
+        def _():
+            for copy in send_row(row, slot, k):
+                copy.start()
     for to in range(2):
         @pl.when(other == to)
         def _():
             send((s, to), to, 3 - to, 4).start()
-    for copy in sends:
-        copy.start()
 
     for me in range(2):
         @pl.when(t == me)
         def _():
             count = 2 + 2 * me
             land[2 + me, 6 - count : 6] = lat[0:count]
-            for slot in (3 - me, 0, 1, 4, 5):
-                send((s, other), me, slot, 4).wait_recv()
+            send((s, other), me, 3 - me, 4).wait_recv()
             send((s, other), 1 - me, 2 + me, 4).wait_send()
-    for copy in sends:
-        copy.wait_send()
-
-    @pl.when(s == 0)
-    def _():
-        land[0:2] = jnp.zeros((2, 6, Q, 128), bf16)
-
-    @pl.when(s == ns - 1)
-    def _():
-        land[4:6] = jnp.zeros((2, 6, Q, 128), bf16)
+            for held, slots in ((s > 0, (0, 1)), (s < ns - 1, (4, 5))):
+                @pl.when(held)
+                def _():
+                    for slot in slots:
+                        send((s, other), me, slot, 4).wait_recv()
+    for held, row, slot, k in rows_held:
+        @pl.when(held)
+        def _():
+            for copy in send_row(row, slot, k):
+                copy.wait_send()
+
+    wide_lane = lax.broadcasted_iota(jnp.int32, (Q, 128), 1)
+    for p in range(4):
+        for f in range(6):
+            beside = jnp.where(
+                wide_lane < 64, land[p + 2, f].astype(f32), land[p, f].astype(f32)
+            ).astype(bf16)
+            windows[p, f] = jnp.concatenate([land[p + 1, f], beside], axis=1)
 
 
 def decoder_kernel(
-    lat_ref, win_ref, bin_ref, gain_ref, wmid_ref, bmid_ref, wup_ref, bup_ref, out_ref,
-    land, win, vectors, wm, wu, wp, windows, comps, skip, staged, mixed, pending, fine,
+    windows_ref, win_ref, bin_ref, gain_ref, wmid_ref, bmid_ref, wup_ref, bup_ref, out_ref,
+    windows, win, wp, vectors, wm, wu, comps, skip, staged, mixed, pending, fine,
     wrow, wphase, spread, phases, lsem, wsem, vsem, msem, usem, osem,
 ):
     s, t = lax.axis_index("space"), lax.axis_index("tm")
     ns = lax.axis_size("space")
-    lat_load = pltpu.make_async_copy(lat_ref, land, lsem)
-    lat_load.start()
-    others = [pltpu.make_async_copy(win_ref, win, wsem)]
+    others = [
+        pltpu.make_async_copy(windows_ref, windows, lsem), pltpu.make_async_copy(win_ref, win, wsem)
+    ]
     for n, ref in enumerate((bin_ref, gain_ref, bmid_ref, bup_ref)):
         others.append(pltpu.make_async_copy(ref, vectors.at[n], vsem.at[n]))
-    mids = [pltpu.make_async_copy(wmid_ref.at[i], wm.at[i], msem.at[i]) for i in range(3)]
-    up_load = pltpu.make_async_copy(wup_ref, wu, usem)
-    for load in others + mids + [up_load]:
+    for load in others:
         load.start()
 
-    wp[...] = jnp.zeros(wp.shape, bf16)
     to = lax.broadcasted_iota(jnp.int32, (256, 256), 0)
     at = lax.broadcasted_iota(jnp.int32, (256, 256), 1)
     spread[...] = jnp.where(
         to == 4 * (at % 64) + 2 * ((at // 64) % 2) + at // 128, 1.0, 0.0
     ).astype(bf16)
+
+    wp[...] = jnp.zeros(wp.shape, bf16)
     for load in others:
         load.wait()
+    mids = [pltpu.make_async_copy(wmid_ref.at[i], wm.at[i], msem.at[i]) for i in range(3)]
+    up_load = pltpu.make_async_copy(wup_ref, wu, usem)
+    for load in mids + [up_load]:
+        load.start()
     for i in range(3):
         for j in range(3):
             block = win[i, j]
@@ -213,14 +232,6 @@
                 for b in range(2):
                     at = i * 256 + ((a + j - 1) % 4) * 64 + b * 16
                     wp[at : at + 48, (2 * a + b) * CH : (2 * a + b + 1) * CH] = block
-    lat_load.wait()
-    lane = lax.broadcasted_iota(jnp.int32, (Q, 128), 1)
-    for p in range(4):
-        for f in range(6):
-            beside = jnp.where(
-                lane < 64, land[p + 2, f].astype(f32), land[p, f].astype(f32)
-            ).astype(bf16)
-            windows[p, f] = jnp.concatenate([land[p + 1, f], beside], axis=1)
 
     bias_first, half_gain = vectors[0], 0.5 * vectors[1]
     bias_mid, bias_up = vectors[2], vectors[3]
@@ -268,11 +279,13 @@
                 + middle[r * Q : (r + 1) * Q]
                 + bias_mid[:, cols]
             ) * held
-            fine[f, r, 1 + b, :, cols] = value.astype(bf16)
-            if b == 0:
-                fine[f, r, 3, :, cols] = moved_up(value).astype(bf16)
-            else:
-                fine[f, r, 0, :, cols] = moved_down(value).astype(bf16)
+            rounded = value.astype(bf16)
+            fine[f, r, b, :, cols] = rounded
+            if b == 1:
+                odd, even = rounded.astype(f32), fine[f, r, 0, :, cols].astype(f32)
+                fine[f, r, 2, :, cols] = (even - moved_down(odd)).astype(bf16)
+                fine[f, r, 3, :, cols] = (odd - even).astype(bf16)
+                fine[f, r, 4, :, cols] = (moved_up(even) - odd).astype(bf16)
 
     def phase_weights(a):
         both = (wu.at[1], wu.at[2]) if a == 0 else (wu.at[0], wu.at[1])
@@ -281,8 +294,8 @@
         for i in range(2):
             held = alone if i == a else wrow
             k0, k1, k2 = [held[k * CH : (k + 1) * CH] for k in range(3)]
-            for n, value in enumerate((k0, k1 + k2, k0 + k1, k2)):
-                wphase[a, i, n] = value
+            for n, value in enumerate((k0, k0 + k1 + k2, k2)):
+                wphase[a, n, i] = value
 
     for k in range(4):
         if k == 0:
@@ -352,17 +365,20 @@
         for f in range(2):
             for n in range(2):
                 cols = slice(n * 256, (n + 1) * 256)
-                for b in range(2):
+                products = []
+                for kind, at in enumerate((2, 0, 3)):
                     lhs = jnp.concatenate(
                         [
-                            fine[f, a + i : a + i + 4, b + c : b + c + 2].reshape(8 * Q, CH)
+                            fine[f, a + i : a + i + 4, at : at + 2].reshape(8 * Q, CH)
                             for i in range(2)
-                            for c in range(2)
                         ],
                         axis=1,
                     )
-                    rhs = wphase[a, :, 2 * b : 2 * b + 2, :, cols].reshape(4 * CH, 256)
-                    value = jnp.dot(lhs, rhs, preferred_element_type=f32) + bias_up[:, cols]
+                    rhs = wphase[a, kind, :, :, cols].reshape(2 * CH, 256)
+                    products.append(jnp.dot(lhs, rhs, preferred_element_type=f32))
+                first, centre, last = products
+                centre = centre + bias_up[:, cols]
+                for b, value in enumerate((centre - first, centre + last)):
                     phases[f, :, b, :, cols] = value.astype(bf16).reshape(4, 2 * Q, 256)
             if behind is not None:
                 order_lines(*behind)
@@ -380,9 +396,9 @@
     anywhere = pl.BlockSpec(memory_space=pltpu.HBM)
     rows = lambda v: v.reshape(1, -1)
     dma = pltpu.SemaphoreType.DMA
-    latents = pl.pallas_call(
+    windows = pl.pallas_call(
         latent_kernel,
-        out_shape=jax.ShapeDtypeStruct((6, 6, Q, 128), bf16),
+        out_shape=jax.ShapeDtypeStruct((4, 6, Q, 256), bf16),
         in_specs=[anywhere] * 7,
         out_specs=vmem,
         scratch_shapes=[
@@ -395,6 +411,7 @@
             pltpu.VMEM((2, 2, 4, 16, 128), f32),
             pltpu.VMEM((128, 128), f32),
             pltpu.VMEM((4, Q, 128), bf16),
+            pltpu.VMEM((6, 6, Q, 128), bf16),
             dma((4,)), dma((5,)), dma, dma, dma, dma((5,)), dma((6,)),
         ],
         compiler_params=pltpu.CompilerParams(
@@ -410,27 +427,26 @@
         in_specs=[anywhere] * 8,
         out_specs=anywhere,
         scratch_shapes=[
-            pltpu.VMEM((6, 6, Q, 128), bf16),
+            pltpu.VMEM((4, 6, Q, 256), bf16),
             pltpu.VMEM((3, 3, 48, CH), bf16),
+            pltpu.VMEM((768, 4 * CH), bf16),
             pltpu.VMEM((4, 1, CH), f32),
             pltpu.VMEM((3, 3, 3 * CH, CH), bf16),
             pltpu.VMEM((3, 3 * CH, CH), bf16),
-            pltpu.VMEM((768, 4 * CH), bf16),
-            pltpu.VMEM((4, 6, Q, 256), bf16),
             pltpu.VMEM((16, 8, Q, CH), bf16),
             pltpu.VMEM((2, 2, 8, Q, CH), bf16),
             pltpu.VMEM((3, 3 * CH, CH), bf16),
             pltpu.VMEM((2, 3 * CH, CH), bf16),
             pltpu.VMEM((2, 2, 6 * Q, CH), f32),
-            pltpu.VMEM((2, 6, 4, Q, CH), bf16),
+            pltpu.VMEM((2, 6, 5, Q, CH), bf16),
             pltpu.VMEM((3 * CH, CH), bf16),
-            pltpu.VMEM((2, 2, 4, CH, CH), bf16),
+            pltpu.VMEM((2, 3, 2, CH, CH), bf16),
             pltpu.VMEM((256, 256), bf16),
             pltpu.VMEM((2, 4, 2, 2 * Q, CH), bf16),
             dma, dma, dma((4,)), dma((3,)), dma, dma((4,)),
         ],
         compiler_params=pltpu.CompilerParams(vmem_limit_bytes=62 << 20),
-    )(latents, w_in, rows(b_in), rows(gain), w_mid, rows(b_mid), w_up, rows(b_up))
+    )(windows, w_in, rows(b_in), rows(gain), w_mid, rows(b_mid), w_up, rows(b_up))
     return decoded.reshape(2, 8, 256, CH)
 
 

time: 54.6 us -> 45.7 us (0.84)
  the two profiles are of different devices: /device:TPU:1 before, /device:TPU:96 now
where the time goes in v2:
time: 45.7 us; the launch traced here: 45.1 us
  Pallas kernels  43.7 us (96%)
  between operations  1.49 us (3%)
    pallas_call x1, Pallas kernels, on_device(): pl.pallas_call(decoder_kernel, out_shape=jax.ShapeDtypeStruct((2, 4, 2, 4...  28.4 us
    pallas_call x1, Pallas kernels, on_device(): pl.pallas_call(latent_kernel, out_shape=jax.ShapeDtypeStruct((4, 6, Q, 25...  15.2 us

profile of v2, /device:TPU:96, one launch (start us, length us, event | category | flops | bytes accessed | tf_op | source)
XLA Modules:
  0.0 45.1 jit_solution(351355529277153452)
XLA Ops:
  1.3 15.2 %shard_map.136.windows_ref = bf16[4,6,64,256]{3,2,1,0:T(8,128)(2,1)} custom-call(bf16[2,4,64,4096]{3,2,1,0:T(8,128)(2,1)} %h_ref.1, f32[2,4096]{1,0:T(2,128)} %mod_ref.1, bf16[64,4096]{1,0:T(8,128)(2,1)} %bitcast.12, f32[1,64]{1,0:T(1,128)} %bitcast.18, f32[1,1]{1,0:T(1,128)} %bitcast.10.g_ref, f32[1,1]{1,0:T(1,128)} %bitcast.11.sigma_ref, ...), custom_call_target="tpu_custom_call" | custom-call | tf_op jit(solution)/shard_map/pallas_call | solution.py:399
  16.5 28.4 %shard_map.137 = bf16[2,4,2,4,64,512]{5,4,3,2,1,0:T(8,128)(2,1)} custom-call(bf16[4,6,64,256]{3,2,1,0:T(8,128)(2,1)} %shard_map.136.windows_ref, bf16[3,3,48,512]{3,2,1,0:T(8,128)(2,1)} %win_ref.1, f32[1,512]{1,0:T(1,128)} %bitcast.14, f32[1,512]{1,0:T(1,128)} %bitcast.15, bf16[3,3,1536,512]{3,2,1,0:T(8,128)(2,1)} %wmid_ref.1, f32[1,512]{1,0:T(1,128)} %bitcast.16, ...), custom_call_target="tpu_custom_call" | custom-call | tf_op jit(solution)/shard_map/pallas_call | solution.py:424

commit v3 on v2

--- a/solution.py
+++ b/solution.py
@@ -12,6 +12,7 @@
 bf16, f32 = jnp.bfloat16, jnp.float32
 CH = 512
 Q = 64
+NT = (((1,), (1,)), ((), ()))
 
 
 def moved_down(x):
@@ -25,8 +26,8 @@
 
 
 def latent_kernel(
-    h_ref, mod_ref, w_ref, b_ref, g_ref, sigma_ref, x_ref, windows,
-    hbuf, wbuf, mod, wmat, bias_in, scalars, xall, xt, lat, land,
+    h_ref, mod_ref, w_ref, tail_ref, x_ref, windows,
+    hbuf, wbuf, mod, wmat, tail, xall, xt, lat, land, wide,
     hsem, ssmall, xlocal, xsend, xrecv, ssem, rsem,
 ):
     s, t = lax.axis_index("space"), lax.axis_index("tm")
@@ -35,18 +36,19 @@
     after, before = s + 1, s - 1
 
     small = []
-    for n, (a, b) in enumerate(
-        ((w_ref, wbuf), (mod_ref, mod), (b_ref, bias_in), (g_ref, scalars.at[0]), (sigma_ref, scalars.at[1]))
-    ):
+    for n, (a, b) in enumerate(((w_ref, wbuf), (mod_ref, mod), (tail_ref, tail))):
         load = pltpu.make_async_copy(a, b, ssmall.at[n])
         load.start()
         small.append(load)
     loads = []
     for f in range(4):
-        load = pltpu.make_async_copy(h_ref.at[:, f], hbuf.at[f], hsem.at[f])
-        load.start()
-        loads.append(load)
-    x_load = pltpu.make_async_copy(x_ref, xall.at[t], xlocal)
+        for k in range(2):
+            load = pltpu.make_async_copy(
+                h_ref.at[k, f], hbuf.at[(2 * f + k) * Q : (2 * f + k + 1) * Q], hsem.at[2 * f + k]
+            )
+            load.start()
+            loads.append(load)
+    x_load = pltpu.make_async_copy(x_ref.at[:, pl.ds(2 * t, 2)], xall.at[t], xlocal)
     x_load.start()
 
     land[...] = jnp.zeros(land.shape, bf16)
@@ -62,18 +64,14 @@
         load.wait()
     scale = 1.0 + mod[1:2, :]
     shift = mod[0:1, :]
-    wide = wbuf[...].astype(f32)
-    ordered = jnp.concatenate(
-        [wide[block * 16 : block * 16 + 16] for block in (0, 2, 1, 3)], axis=0
-    )
-    both = jnp.concatenate([ordered * scale, ordered], axis=0)
-    for k in range(8):
-        at = slice(k * 512, (k + 1) * 512)
-        wmat[at] = jnp.transpose(both[:, at]).astype(bf16)
+    for n, block in enumerate((0, 2, 1, 3)):
+        part = wbuf[block * 16 : block * 16 + 16]
+        wmat[n * 16 : n * 16 + 16] = (part.astype(f32) * scale).astype(bf16)
+        wmat[64 + n * 16 : 80 + n * 16] = part
     shift_hi = shift.astype(bf16)
     shift_lo = (shift - shift_hi.astype(f32)).astype(bf16)
     row = lax.broadcasted_iota(jnp.int32, (16, shift.shape[1]), 0)
-    sums = jnp.where(
+    hbuf[8 * Q :] = jnp.where(
         row == 0,
         1.0,
         jnp.where(
@@ -84,75 +82,60 @@
     source = ((lane // 16) % 2) * 32 + (lane // 32) * 16 + lane % 16
     one_hot = (lax.broadcasted_iota(jnp.int32, (Q, Q), 0) == source).astype(f32)
     bias = jnp.dot(
-        jnp.broadcast_to(bias_in[...], (8, Q)), one_hot,
+        jnp.broadcast_to(tail[:, :Q], (8, Q)), one_hot,
         preferred_element_type=f32, precision=lax.Precision.HIGHEST,
     )[0:1]
-
-    totals = jnp.dot(sums, wmat[...], preferred_element_type=f32)
-    column_sum = totals[0:1, :Q]
-    constant = totals[1:2, Q:] + totals[2:3, Q:] + bias
+    guidance, sigma = tail[:, Q : Q + 1], tail[:, Q + 1 : Q + 2]
 
     pl.semaphore_wait(
         barrier, 1 + 2 * (s > 0).astype(jnp.int32) + 2 * (s < ns - 1).astype(jnp.int32)
     )
     x_copy = pltpu.make_async_remote_copy(
-        src_ref=x_ref, dst_ref=xall.at[t], send_sem=xsend, recv_sem=xrecv,
-        device_id=(s, other), device_id_type=MESH,
+        src_ref=x_ref.at[:, pl.ds(2 * other, 2)], dst_ref=xall.at[t], send_sem=xsend,
+        recv_sem=xrecv, device_id=(s, other), device_id_type=MESH,
     )
     x_copy.start()
 
-    guidance, sigma = scalars[0], scalars[1]
+    for load in loads:
+        load.wait()
+    product = lax.dot_general(hbuf[...], wmat[...], NT, preferred_element_type=f32)
+    statistics = []
+    for f in range(4):
+        rows = hbuf[2 * f * Q : 2 * (f + 1) * Q]
+        pivot = rows[:, 0:1].astype(f32)
+        first, second = jnp.zeros((2 * Q, 128), f32), jnp.zeros((2 * Q, 128), f32)
+        for k in range(32):
+            part = rows[:, k * 128 : (k + 1) * 128].astype(f32) - pivot
+            first = first + part
+            second = second + part * part
+        offset = jnp.sum(first, axis=1, keepdims=True) * (1.0 / 4096)
+        spread = jnp.sum(second, axis=1, keepdims=True) * (1.0 / 4096) - offset * offset
+        statistics.append((pivot + offset, lax.rsqrt(jnp.maximum(spread, 0.0) + norm_eps)))
+    column_sum = product[8 * Q : 8 * Q + 1, :Q]
+    constant = product[8 * Q + 1 : 8 * Q + 2, Q:] + product[8 * Q + 2 : 8 * Q + 3, Q:] + bias
     predictions = []
-    for pair in range(2):
-        loads[2 * pair].wait()
-        loads[2 * pair + 1].wait()
-        product = jnp.dot(
-            hbuf[2 * pair : 2 * pair + 2].reshape(4 * Q, 4096), wmat[...],
-            preferred_element_type=f32,
-        )
-        for f in range(2):
-            rows = hbuf[2 * pair + f].reshape(2 * Q, 4096)
-            pivot = rows[:, 0:1].astype(f32)
-            first, second = jnp.zeros((2 * Q, 128), f32), jnp.zeros((2 * Q, 128), f32)
-            for k in range(32):
-                part = rows[:, k * 128 : (k + 1) * 128].astype(f32) - pivot
-                first = first + part
-                second = second + part * part
-            offset = jnp.sum(first, axis=1, keepdims=True) * (1.0 / 4096)
-            spread = jnp.sum(second, axis=1, keepdims=True) * (1.0 / 4096) - offset * offset
-            inverse = lax.rsqrt(jnp.maximum(spread, 0.0) + norm_eps)
-            own = product[2 * f * Q : 2 * (f + 1) * Q, :Q]
-            branch = inverse * (own - (pivot + offset) * column_sum)
-            cond, uncond = branch[:Q], branch[Q:]
-            predictions.append(uncond + guidance * (cond - uncond) + constant)
+    for f in range(4):
+        centre, inverse = statistics[f]
+        branch = inverse * (product[2 * f * Q : 2 * (f + 1) * Q, :Q] - centre * column_sum)
+        cond, uncond = branch[:Q], branch[Q:]
+        predictions.append(uncond + guidance * (cond - uncond) + constant)
 
     x_load.wait()
     x_copy.wait()
-    xt[...] = jnp.transpose(
-        jnp.concatenate([xall[f // 2, f % 2, 2 * t + a] for f in range(4) for a in range(2)], axis=0)
-    )
+    xt[...] = jnp.transpose(xall[...].reshape(128, 128))
     even, odd = xt[pl.ds(0, Q, stride=2), :], xt[pl.ds(1, Q, stride=2), :]
-    position = lax.broadcasted_iota(jnp.int32, (Q, Q), 0)
-    compact = []
-    for f in range(4):
-        at = slice(32 * f, 32 * f + 32)
-        noisy = jnp.concatenate([even[:, at], odd[:, at]], axis=1)
-        latent = noisy - sigma * predictions[f]
-        from_left = jnp.where(position == 0, 0.0, pltpu.roll(latent, 1, 0))
-        from_right = jnp.where(position == Q - 1, 0.0, pltpu.roll(latent, Q - 1, 0))
-        beside = jnp.where(lane < 32, from_right, from_left)
-        compact.append(jnp.concatenate([latent, beside], axis=1).astype(bf16))
-    to = lax.broadcasted_iota(jnp.int32, (128, 128), 1)
-    source = ((to // 16 + 3) % 4) * 32 + (to // 64) * 16 + to % 16
-    widen = (lax.broadcasted_iota(jnp.int32, (128, 128), 0) == source).astype(f32).astype(bf16)
-    lat[...] = jnp.dot(
-        jnp.concatenate(compact, axis=0), widen, preferred_element_type=f32
-    ).astype(bf16).reshape(4, Q, 128)
+    for pair in range(2):
+        latents = []
+        for f in (2 * pair, 2 * pair + 1):
+            at = slice(32 * f, 32 * f + 32)
+            noisy = jnp.concatenate([even[:, at], odd[:, at]], axis=1)
+            latents.append(noisy - sigma * predictions[f])
+        lat[pair] = jnp.concatenate(latents, axis=1).astype(bf16)
 
     def send(peer, to, slot, k):
-        count = 2 + 2 * to
+        count = 1 + to
         return pltpu.make_async_remote_copy(
-            src_ref=lat.at[pl.ds(0, count)], dst_ref=land.at[slot, pl.ds(6 - count, count)],
+            src_ref=lat.at[pl.ds(0, count)], dst_ref=land.at[slot, pl.ds(3 - count, count)],
             send_sem=ssem.at[k], recv_sem=rsem.at[slot], device_id=peer, device_id_type=MESH,
         )
 
@@ -170,11 +153,17 @@
         def _():
             send((s, to), to, 3 - to, 4).start()
 
+    at = lax.broadcasted_iota(jnp.int32, (256, 256), 0)
+    to = lax.broadcasted_iota(jnp.int32, (256, 256), 1)
+    turn = (to // 16 + 3) % 4
+    source = (turn // 2) * 128 + (to // 128) * 64 + (turn % 2) * 32 + ((to // 64) % 2) * 16 + to % 16
+    widen = (at == source).astype(f32).astype(bf16)
+
     for me in range(2):
         @pl.when(t == me)
         def _():
-            count = 2 + 2 * me
-            land[2 + me, 6 - count : 6] = lat[0:count]
+            count = 1 + me
+            land[2 + me, 3 - count : 3] = lat[0:count]
             send((s, other), me, 3 - me, 4).wait_recv()
             send((s, other), 1 - me, 2 + me, 4).wait_send()
             for held, slots in ((s > 0, (0, 1)), (s < ns - 1, (4, 5))):
@@ -188,13 +177,26 @@
             for copy in send_row(row, slot, k):
                 copy.wait_send()
 
+    position = lax.broadcasted_iota(jnp.int32, (Q, 128), 0)
     wide_lane = lax.broadcasted_iota(jnp.int32, (Q, 128), 1)
+    parts = []
+    for p in range(6):
+        for pair in range(3):
+            here = land[p, pair].astype(f32)
+            from_left = jnp.where(position == 0, 0.0, pltpu.roll(here, 1, 0))
+            from_right = jnp.where(position == Q - 1, 0.0, pltpu.roll(here, Q - 1, 0))
+            beside = jnp.where((wide_lane // 32) % 2 == 0, from_right, from_left)
+            parts.append(jnp.concatenate([here, beside], axis=1).astype(bf16))
+    wide[...] = jnp.dot(
+        jnp.concatenate(parts, axis=0), widen, preferred_element_type=f32
+    ).astype(bf16).reshape(6, 3, Q, 256)
     for p in range(4):
         for f in range(6):
+            at = slice(f % 2 * 128, f % 2 * 128 + 128)
             beside = jnp.where(
-                wide_lane < 64, land[p + 2, f].astype(f32), land[p, f].astype(f32)
+                wide_lane < 64, wide[p + 2, f // 2, :, at].astype(f32), wide[p, f // 2, :, at].astype(f32)
             ).astype(bf16)
-            windows[p, f] = jnp.concatenate([land[p + 1, f], beside], axis=1)
+            windows[p, f] = jnp.concatenate([wide[p + 1, f // 2, :, at], beside], axis=1)
 
 
 def decoder_kernel(
@@ -267,7 +269,8 @@
                 comps[4 * k + 3, line] = (even - moved_up(even)).astype(bf16)
         return 0
 
-    lax.fori_loop(0, 4, patch_row, 0)
+    for p in range(4):
+        patch_row(p, 0)
 
     def finish(f, b, n, middle):
         cols = slice(n * 256, (n + 1) * 256)
@@ -399,26 +402,26 @@
     windows = pl.pallas_call(
         latent_kernel,
         out_shape=jax.ShapeDtypeStruct((4, 6, Q, 256), bf16),
-        in_specs=[anywhere] * 7,
+        in_specs=[anywhere] * 5,
         out_specs=vmem,
         scratch_shapes=[
-            pltpu.VMEM((4, 2, Q, 4096), bf16),
+            pltpu.VMEM((8 * Q + 16, 4096), bf16),
             pltpu.VMEM((64, 4096), bf16),
             pltpu.VMEM((2, 4096), f32),
-            pltpu.VMEM((4096, 128), bf16),
-            pltpu.VMEM((1, 64), f32),
-            pltpu.VMEM((2, 1, 1), f32),
-            pltpu.VMEM((2, 2, 4, 16, 128), f32),
+            pltpu.VMEM((128, 4096), bf16),
+            pltpu.VMEM((1, 66), f32),
+            pltpu.VMEM((2, 2, 2, 16, 128), f32),
             pltpu.VMEM((128, 128), f32),
-            pltpu.VMEM((4, Q, 128), bf16),
-            pltpu.VMEM((6, 6, Q, 128), bf16),
-            dma((4,)), dma((5,)), dma, dma, dma, dma((5,)), dma((6,)),
+            pltpu.VMEM((2, Q, 128), bf16),
+            pltpu.VMEM((6, 3, Q, 128), bf16),
+            pltpu.VMEM((6, 3, Q, 256), bf16),
+            dma((8,)), dma((3,)), dma, dma, dma, dma((5,)), dma((6,)),
         ],
         compiler_params=pltpu.CompilerParams(
             collective_id=0, has_side_effects=True, vmem_limit_bytes=60 << 20
         ),
     )(
-        hidden, modulation, w_proj.T, rows(b_proj), rows(guidance), rows(sigma),
+        hidden, modulation, w_proj.T, rows(jnp.concatenate([b_proj, guidance, sigma])),
         jnp.swapaxes(x_noisy, 2, 3),
     )
     decoded = pl.pallas_call(

time: 45.7 us -> 44.6 us (0.976)
  Pallas kernels: 43.7 us -> 41.7 us
  other arithmetic: 0 us -> 1.24 us
    reshape x0 -> x1, other arithmetic: none -> 1.24 us  [on_device(): rows = lambda v: v.reshape(1, -1)]
    pallas_call x1, Pallas kernels: 28.4 us -> 27.4 us  [on_device(): pl.pallas_call(decoder_kernel, out_shape=jax.ShapeDtypeStruct((2, 4, 2, 4...]
    pallas_call x1, Pallas kernels: 15.2 us -> 14.3 us  [on_device(): pl.pallas_call(latent_kernel, out_shape=jax.ShapeDtypeStruct((4, 6, Q, 25...]
where the time goes in v3:
time: 44.6 us; the launch traced here: 44.5 us
  Pallas kernels  41.7 us (93%)
  between operations  1.49 us (3%)
  other arithmetic  1.24 us (3%)
    pallas_call x1, Pallas kernels, on_device(): pl.pallas_call(decoder_kernel, out_shape=jax.ShapeDtypeStruct((2, 4, 2, 4...  27.4 us
    pallas_call x1, Pallas kernels, on_device(): pl.pallas_call(latent_kernel, out_shape=jax.ShapeDtypeStruct((4, 6, Q, 25...  14.3 us
    reshape x1, other arithmetic, on_device(): rows = lambda v: v.reshape(1, -1)  1.24 us

profile of v3, /device:TPU:96, one launch (start us, length us, event | category | flops | bytes accessed | tf_op | source)
XLA Modules:
  0.0 44.5 jit_solution(14977598294965912990)
XLA Ops:
  1.3 1.2 %maximum_bitcast_fusion.tail_ref = f32[1,66]{1,0:T(1,128)} fusion(f32[1]{0:T(128)S(6)} %copy.16, f32[1]{0:T(128)S(6)} %copy.15, f32[64]{0:T(128)} %param.17), kind=kLoop, calls=%fused_computation | loop fusion | flops 132 | bytes 528 | tf_op jit(solution)/shard_map/reshape | solution.py:400
  2.5 14.3 %shard_map.136.windows_ref = bf16[4,6,64,256]{3,2,1,0:T(8,128)(2,1)} custom-call(bf16[2,4,64,4096]{3,2,1,0:T(8,128)(2,1)} %h_ref.1, f32[2,4096]{1,0:T(2,128)} %mod_ref.1, bf16[64,4096]{1,0:T(8,128)(2,1)} %bitcast.9, f32[1,66]{1,0:T(1,128)} %maximum_bitcast_fusion.tail_ref, f32[2,4,16,128]{3,2,1,0:T(8,128)} %bitcast.10), custom_call_target="tpu_custom_call" | custom-call | tf_op jit(solution)/shard_map/pallas_call | solution.py:402
  16.9 27.4 %shard_map.137 = bf16[2,4,2,4,64,512]{5,4,3,2,1,0:T(8,128)(2,1)} custom-call(bf16[4,6,64,256]{3,2,1,0:T(8,128)(2,1)} %shard_map.136.windows_ref, bf16[3,3,48,512]{3,2,1,0:T(8,128)(2,1)} %win_ref.1, f32[1,512]{1,0:T(1,128)} %bitcast.11, f32[1,512]{1,0:T(1,128)} %bitcast.12, bf16[3,3,1536,512]{3,2,1,0:T(8,128)(2,1)} %wmid_ref.1, f32[1,512]{1,0:T(1,128)} %bitcast.13, ...), custom_call_target="tpu_custom_call" | custom-call | tf_op jit(solution)/shard_map/pallas_call | solution.py:427

commit v4 on v3

--- a/solution.py
+++ b/solution.py
@@ -26,8 +26,8 @@
 
 
 def latent_kernel(
-    h_ref, mod_ref, w_ref, tail_ref, x_ref, windows,
-    hbuf, wbuf, mod, wmat, tail, xall, xt, lat, land, wide,
+    h_ref, mod_ref, w_ref, b_ref, g_ref, sigma_ref, x_ref, windows,
+    hbuf, wbuf, mod, wmat, bias_in, scalars, xall, xt, lat, land, wide,
     hsem, ssmall, xlocal, xsend, xrecv, ssem, rsem,
 ):
     s, t = lax.axis_index("space"), lax.axis_index("tm")
@@ -36,7 +36,9 @@
     after, before = s + 1, s - 1
 
     small = []
-    for n, (a, b) in enumerate(((w_ref, wbuf), (mod_ref, mod), (tail_ref, tail))):
+    for n, (a, b) in enumerate(
+        ((w_ref, wbuf), (mod_ref, mod), (b_ref, bias_in), (g_ref, scalars.at[0]), (sigma_ref, scalars.at[1]))
+    ):
         load = pltpu.make_async_copy(a, b, ssmall.at[n])
         load.start()
         small.append(load)
@@ -59,6 +61,15 @@
         def _():
             for k in range(2):
                 pl.semaphore_signal(barrier, inc=1, device_id=(row, k), device_id_type=MESH)
+
+    pl.semaphore_wait(
+        barrier, 1 + 2 * (s > 0).astype(jnp.int32) + 2 * (s < ns - 1).astype(jnp.int32)
+    )
+    x_copy = pltpu.make_async_remote_copy(
+        src_ref=x_ref.at[:, pl.ds(2 * other, 2)], dst_ref=xall.at[t], send_sem=xsend,
+        recv_sem=xrecv, device_id=(s, other), device_id_type=MESH,
+    )
+    x_copy.start()
 
     for load in small:
         load.wait()
@@ -82,19 +93,10 @@
     source = ((lane // 16) % 2) * 32 + (lane // 32) * 16 + lane % 16
     one_hot = (lax.broadcasted_iota(jnp.int32, (Q, Q), 0) == source).astype(f32)
     bias = jnp.dot(
-        jnp.broadcast_to(tail[:, :Q], (8, Q)), one_hot,
+        jnp.broadcast_to(bias_in[...], (8, Q)), one_hot,
         preferred_element_type=f32, precision=lax.Precision.HIGHEST,
     )[0:1]
-    guidance, sigma = tail[:, Q : Q + 1], tail[:, Q + 1 : Q + 2]
-
-    pl.semaphore_wait(
-        barrier, 1 + 2 * (s > 0).astype(jnp.int32) + 2 * (s < ns - 1).astype(jnp.int32)
-    )
-    x_copy = pltpu.make_async_remote_copy(
-        src_ref=x_ref.at[:, pl.ds(2 * other, 2)], dst_ref=xall.at[t], send_sem=xsend,
-        recv_sem=xrecv, device_id=(s, other), device_id_type=MESH,
-    )
-    x_copy.start()
+    guidance, sigma = scalars[0], scalars[1]
 
     for load in loads:
         load.wait()
@@ -181,7 +183,7 @@
     wide_lane = lax.broadcasted_iota(jnp.int32, (Q, 128), 1)
     parts = []
     for p in range(6):
-        for pair in range(3):
+        for pair in (1, 2):
             here = land[p, pair].astype(f32)
             from_left = jnp.where(position == 0, 0.0, pltpu.roll(here, 1, 0))
             from_right = jnp.where(position == Q - 1, 0.0, pltpu.roll(here, Q - 1, 0))
@@ -189,20 +191,20 @@
             parts.append(jnp.concatenate([here, beside], axis=1).astype(bf16))
     wide[...] = jnp.dot(
         jnp.concatenate(parts, axis=0), widen, preferred_element_type=f32
-    ).astype(bf16).reshape(6, 3, Q, 256)
+    ).astype(bf16).reshape(6, 2, Q, 256)
     for p in range(4):
-        for f in range(6):
+        windows[p, 0:2] = jnp.zeros((2, Q, 256), bf16)
+        for f in range(2, 6):
             at = slice(f % 2 * 128, f % 2 * 128 + 128)
-            beside = jnp.where(
-                wide_lane < 64, wide[p + 2, f // 2, :, at].astype(f32), wide[p, f // 2, :, at].astype(f32)
-            ).astype(bf16)
-            windows[p, f] = jnp.concatenate([wide[p + 1, f // 2, :, at], beside], axis=1)
+            above, own, below = [wide[p + k, f // 2 - 1, :, at] for k in range(3)]
+            beside = jnp.where(wide_lane < 64, below.astype(f32), above.astype(f32)).astype(bf16)
+            windows[p, f] = jnp.concatenate([own, beside], axis=1)
 
 
 def decoder_kernel(
     windows_ref, win_ref, bin_ref, gain_ref, wmid_ref, bmid_ref, wup_ref, bup_ref, out_ref,
     windows, win, wp, vectors, wm, wu, comps, skip, staged, mixed, pending, fine,
-    wrow, wphase, spread, phases, lsem, wsem, vsem, msem, usem, osem,
+    wrow, wphase, stage, lsem, wsem, vsem, msem, usem, osem,
 ):
     s, t = lax.axis_index("space"), lax.axis_index("tm")
     ns = lax.axis_size("space")
@@ -213,12 +215,6 @@
         others.append(pltpu.make_async_copy(ref, vectors.at[n], vsem.at[n]))
     for load in others:
         load.start()
-
-    to = lax.broadcasted_iota(jnp.int32, (256, 256), 0)
-    at = lax.broadcasted_iota(jnp.int32, (256, 256), 1)
-    spread[...] = jnp.where(
-        to == 4 * (at % 64) + 2 * ((at // 64) % 2) + at // 128, 1.0, 0.0
-    ).astype(bf16)
 
     wp[...] = jnp.zeros(wp.shape, bf16)
     for load in others:
@@ -348,20 +344,18 @@
 
     writes = []
 
-    def order_lines(f, a):
-        lines = jnp.dot(
-            spread[...],
-            jnp.concatenate([phases[f, r].reshape(256, CH) for r in range(4)], axis=1),
-            preferred_element_type=f32,
-        ).astype(bf16)
-        base = 8 * a + 4 * f
+    def write_lines(f, a):
         for r in range(4):
-            comps[base + r, 0:4] = lines[:, r * CH : (r + 1) * CH].reshape(4, Q, CH)
-        write = pltpu.make_async_copy(
-            comps.at[base : base + 4, 0:4], out_ref.at[f, :, a], osem.at[2 * a + f]
-        )
-        write.start()
-        writes.append(write)
+            line = 8 * a + 4 * f + r
+            for g in range(4):
+                comps[line, 0:4, :, g * 128 : (g + 1) * 128] = stage[f, r, g].astype(bf16).reshape(
+                    4, Q, 128
+                )
+            write = pltpu.make_async_copy(
+                comps.at[line, 0:4], out_ref.at[f, r, a], osem.at[line]
+            )
+            write.start()
+            writes.append(write)
 
     behind = None
     for a in range(2):
@@ -382,11 +376,17 @@
                 first, centre, last = products
                 centre = centre + bias_up[:, cols]
                 for b, value in enumerate((centre - first, centre + last)):
-                    phases[f, :, b, :, cols] = value.astype(bf16).reshape(4, 2 * Q, 256)
+                    for r in range(4):
+                        for side in range(2):
+                            at = (2 * r + side) * Q
+                            for g in range(2):
+                                stage[f, r, 2 * n + g, pl.ds(2 * side + b, Q, stride=4), :] = value[
+                                    at : at + Q, g * 128 : (g + 1) * 128
+                                ]
             if behind is not None:
-                order_lines(*behind)
+                write_lines(*behind)
             behind = (f, a)
-    order_lines(*behind)
+    write_lines(*behind)
     for write in writes:
         write.wait()
 
@@ -402,26 +402,27 @@
     windows = pl.pallas_call(
         latent_kernel,
         out_shape=jax.ShapeDtypeStruct((4, 6, Q, 256), bf16),
-        in_specs=[anywhere] * 5,
+        in_specs=[anywhere] * 7,
         out_specs=vmem,
         scratch_shapes=[
             pltpu.VMEM((8 * Q + 16, 4096), bf16),
             pltpu.VMEM((64, 4096), bf16),
             pltpu.VMEM((2, 4096), f32),
             pltpu.VMEM((128, 4096), bf16),
-            pltpu.VMEM((1, 66), f32),
+            pltpu.VMEM((1, 64), f32),
+            pltpu.VMEM((2, 1, 1), f32),
             pltpu.VMEM((2, 2, 2, 16, 128), f32),
             pltpu.VMEM((128, 128), f32),
             pltpu.VMEM((2, Q, 128), bf16),
             pltpu.VMEM((6, 3, Q, 128), bf16),
-            pltpu.VMEM((6, 3, Q, 256), bf16),
-            dma((8,)), dma((3,)), dma, dma, dma, dma((5,)), dma((6,)),
+            pltpu.VMEM((6, 2, Q, 256), bf16),
+            dma((8,)), dma((5,)), dma, dma, dma, dma((5,)), dma((6,)),
         ],
         compiler_params=pltpu.CompilerParams(
             collective_id=0, has_side_effects=True, vmem_limit_bytes=60 << 20
         ),
     )(
-        hidden, modulation, w_proj.T, rows(jnp.concatenate([b_proj, guidance, sigma])),
+        hidden, modulation, w_proj.T, rows(b_proj), rows(guidance), rows(sigma),
         jnp.swapaxes(x_noisy, 2, 3),
     )
     decoded = pl.pallas_call(
@@ -444,9 +445,8 @@
             pltpu.VMEM((2, 6, 5, Q, CH), bf16),
             pltpu.VMEM((3 * CH, CH), bf16),
             pltpu.VMEM((2, 3, 2, CH, CH), bf16),
-            pltpu.VMEM((256, 256), bf16),
-            pltpu.VMEM((2, 4, 2, 2 * Q, CH), bf16),
-            dma, dma, dma((4,)), dma((3,)), dma, dma((4,)),
+            pltpu.VMEM((2, 4, 4, 256, 128), f32),
+            dma, dma, dma((4,)), dma((3,)), dma, dma((16,)),
         ],
         compiler_params=pltpu.CompilerParams(vmem_limit_bytes=62 << 20),
     )(windows, w_in, rows(b_in), rows(gain), w_mid, rows(b_mid), w_up, rows(b_up))

time: 44.6 us -> 42.6 us (0.955)
  other arithmetic: 1.24 us -> 0 us
  Pallas kernels: 41.7 us -> 40.9 us
    reshape x1 -> x0, other arithmetic: 1.24 us -> none  [on_device(): rows = lambda v: v.reshape(1, -1)]
    pallas_call x1, Pallas kernels: 27.4 us -> 26.6 us  [on_device(): pl.pallas_call(decoder_kernel, out_shape=jax.ShapeDtypeStruct((2, 4, 2, 4...]
where the time goes in v4:
time: 42.6 us; the launch traced here: 42.4 us
  Pallas kernels  40.9 us (96%)
  between operations  1.49 us (3%)
    pallas_call x1, Pallas kernels, on_device(): pl.pallas_call(decoder_kernel, out_shape=jax.ShapeDtypeStruct((2, 4, 2, 4...  26.6 us
    pallas_call x1, Pallas kernels, on_device(): pl.pallas_call(latent_kernel, out_shape=jax.ShapeDtypeStruct((4, 6, Q, 25...  14.3 us

profile of v4, /device:TPU:96, one launch (start us, length us, event | category | flops | bytes accessed | tf_op | source)
XLA Modules:
  0.0 42.4 jit_solution(17646085095597489714)
XLA Ops:
  1.3 14.3 %shard_map.136.windows_ref = bf16[4,6,64,256]{3,2,1,0:T(8,128)(2,1)} custom-call(bf16[2,4,64,4096]{3,2,1,0:T(8,128)(2,1)} %h_ref.1, f32[2,4096]{1,0:T(2,128)} %mod_ref.1, bf16[64,4096]{1,0:T(8,128)(2,1)} %bitcast.12, f32[1,64]{1,0:T(1,128)} %bitcast.18, f32[1,1]{1,0:T(1,128)} %bitcast.10.g_ref, f32[1,1]{1,0:T(1,128)} %bitcast.11.sigma_ref, ...), custom_call_target="tpu_custom_call" | custom-call | tf_op jit(solution)/shard_map/pallas_call | solution.py:402
  15.6 26.6 %shard_map.137 = bf16[2,4,2,4,64,512]{5,4,3,2,1,0:T(8,128)(2,1)} custom-call(bf16[4,6,64,256]{3,2,1,0:T(8,128)(2,1)} %shard_map.136.windows_ref, bf16[3,3,48,512]{3,2,1,0:T(8,128)(2,1)} %win_ref.1, f32[1,512]{1,0:T(1,128)} %bitcast.14, f32[1,512]{1,0:T(1,128)} %bitcast.15, bf16[3,3,1536,512]{3,2,1,0:T(8,128)(2,1)} %wmid_ref.1, f32[1,512]{1,0:T(1,128)} %bitcast.16, ...), custom_call_target="tpu_custom_call" | custom-call | tf_op jit(solution)/shard_map/pallas_call | solution.py:428

commit v5 on v4

--- a/solution.py
+++ b/solution.py
@@ -73,29 +73,24 @@
 
     for load in small:
         load.wait()
-    scale = 1.0 + mod[1:2, :]
-    shift = mod[0:1, :]
-    for n, block in enumerate((0, 2, 1, 3)):
-        part = wbuf[block * 16 : block * 16 + 16]
-        wmat[n * 16 : n * 16 + 16] = (part.astype(f32) * scale).astype(bf16)
-        wmat[64 + n * 16 : 80 + n * 16] = part
-    shift_hi = shift.astype(bf16)
-    shift_lo = (shift - shift_hi.astype(f32)).astype(bf16)
-    row = lax.broadcasted_iota(jnp.int32, (16, shift.shape[1]), 0)
-    hbuf[8 * Q :] = jnp.where(
-        row == 0,
-        1.0,
-        jnp.where(
-            row == 1, shift_hi.astype(f32), jnp.where(row == 2, shift_lo.astype(f32), 0.0)
-        ),
-    ).astype(bf16)
-    lane = lax.broadcasted_iota(jnp.int32, (Q, Q), 1)
-    source = ((lane // 16) % 2) * 32 + (lane // 32) * 16 + lane % 16
-    one_hot = (lax.broadcasted_iota(jnp.int32, (Q, Q), 0) == source).astype(f32)
-    bias = jnp.dot(
-        jnp.broadcast_to(bias_in[...], (8, Q)), one_hot,
-        preferred_element_type=f32, precision=lax.Precision.HIGHEST,
-    )[0:1]
+    scale, shift = 1.0 + mod[1:2, :], mod[0:1, :]
+    scaled_sum, shift_sum = jnp.zeros((Q, 128), f32), jnp.zeros((Q, 128), f32)
+    for k in range(32):
+        at = slice(k * 128, (k + 1) * 128)
+        plain = jnp.concatenate(
+            [wbuf[n * 16 : n * 16 + 16, at].astype(f32) for n in (0, 2, 1, 3)], axis=0
+        )
+        scaled = (plain * scale[:, at]).astype(bf16)
+        wmat[:, at] = scaled
+        scaled_sum = scaled_sum + scaled.astype(f32)
+        shift_sum = shift_sum + plain * shift[:, at]
+    totals = jnp.sum(
+        jnp.transpose(jnp.concatenate([scaled_sum, shift_sum], axis=0)), axis=0, keepdims=True
+    )
+    bias = jnp.concatenate(
+        [bias_in[:, n * 16 : n * 16 + 16] for n in (0, 2, 1, 3)], axis=1
+    )
+    column_sum, constant = totals[:, :Q], totals[:, Q:] + bias
     guidance, sigma = scalars[0], scalars[1]
 
     for load in loads:
@@ -113,12 +108,10 @@
         offset = jnp.sum(first, axis=1, keepdims=True) * (1.0 / 4096)
         spread = jnp.sum(second, axis=1, keepdims=True) * (1.0 / 4096) - offset * offset
         statistics.append((pivot + offset, lax.rsqrt(jnp.maximum(spread, 0.0) + norm_eps)))
-    column_sum = product[8 * Q : 8 * Q + 1, :Q]
-    constant = product[8 * Q + 1 : 8 * Q + 2, Q:] + product[8 * Q + 2 : 8 * Q + 3, Q:] + bias
     predictions = []
     for f in range(4):
         centre, inverse = statistics[f]
-        branch = inverse * (product[2 * f * Q : 2 * (f + 1) * Q, :Q] - centre * column_sum)
+        branch = inverse * (product[2 * f * Q : 2 * (f + 1) * Q] - centre * column_sum)
         cond, uncond = branch[:Q], branch[Q:]
         predictions.append(uncond + guidance * (cond - uncond) + constant)
 
@@ -193,23 +186,22 @@
         jnp.concatenate(parts, axis=0), widen, preferred_element_type=f32
     ).astype(bf16).reshape(6, 2, Q, 256)
     for p in range(4):
-        windows[p, 0:2] = jnp.zeros((2, Q, 256), bf16)
         for f in range(2, 6):
             at = slice(f % 2 * 128, f % 2 * 128 + 128)
             above, own, below = [wide[p + k, f // 2 - 1, :, at] for k in range(3)]
             beside = jnp.where(wide_lane < 64, below.astype(f32), above.astype(f32)).astype(bf16)
-            windows[p, f] = jnp.concatenate([own, beside], axis=1)
+            windows[p, f - 2] = jnp.concatenate([own, beside], axis=1)
 
 
 def decoder_kernel(
     windows_ref, win_ref, bin_ref, gain_ref, wmid_ref, bmid_ref, wup_ref, bup_ref, out_ref,
-    windows, win, wp, vectors, wm, wu, comps, skip, staged, mixed, pending, fine,
-    wrow, wphase, stage, lsem, wsem, vsem, msem, usem, osem,
+    windows, win, wp, vectors, wm, wu, comps, skip, turned, mixed, last, pending, fine, wphase, stage, lsem, wsem, vsem, msem, usem, osem,
 ):
     s, t = lax.axis_index("space"), lax.axis_index("tm")
     ns = lax.axis_size("space")
     others = [
-        pltpu.make_async_copy(windows_ref, windows, lsem), pltpu.make_async_copy(win_ref, win, wsem)
+        pltpu.make_async_copy(windows_ref, windows.at[:, 2:6], lsem),
+        pltpu.make_async_copy(win_ref, win, wsem),
     ]
     for n, ref in enumerate((bin_ref, gain_ref, bmid_ref, bup_ref)):
         others.append(pltpu.make_async_copy(ref, vectors.at[n], vsem.at[n]))
@@ -217,6 +209,12 @@
         load.start()
 
     wp[...] = jnp.zeros(wp.shape, bf16)
+    windows[:, 0:2] = jnp.zeros((4, 2, Q, 256), bf16)
+    for n in range(2):
+        for k in range(4):
+            for b in range(2):
+                turned[n, k, b, 0:8] = jnp.zeros((8, CH), f32)
+                turned[n, k, b, 8 + Q :] = jnp.zeros((8, CH), f32)
     for load in others:
         load.wait()
     mids = [pltpu.make_async_copy(wmid_ref.at[i], wm.at[i], msem.at[i]) for i in range(3)]
@@ -233,40 +231,37 @@
 
     bias_first, half_gain = vectors[0], 0.5 * vectors[1]
     bias_mid, bias_up = vectors[2], vectors[3]
-    frame = lax.broadcasted_iota(jnp.int32, (4 * Q, 1), 0) // Q
-    frame_held = jnp.logical_or(frame >= 2, t > 0)
-
-    def patch_row(p, _):
+    for p in range(4):
         lhs = jnp.concatenate(
             [windows[p, i : i + 4].reshape(4 * Q, 256) for i in range(3)], axis=1
         )
         for a in range(2):
             line = 2 * p + a
             held = jnp.logical_and(4 * s - 2 + line >= 0, 4 * s - 2 + line < 4 * ns)
-            mask = jnp.where(jnp.logical_and(frame_held, held), 1.0, 0.0)
-            sides = []
+            own = jnp.where(held, 1.0, 0.0)
+            earlier = jnp.where(jnp.logical_and(held, t > 0), 1.0, 0.0)
             for b in range(2):
                 column = (2 * a + b) * CH
-                value = jnp.dot(
-                    lhs, wp[:, column : column + CH], preferred_element_type=f32
-                ) + bias_first
-                for f in range(2):
-                    skip[f, b, line] = value[(2 + f) * Q : (3 + f) * Q].astype(bf16)
-                power = jnp.mean(value * value, axis=1, keepdims=True)
-                half = value * (lax.rsqrt(power + norm_eps) * mask) * half_gain
-                active = half * jnp.tanh(half) + half
-                a0, a1, a2, a3 = [active[f * Q : (f + 1) * Q] for f in range(4)]
-                sides.append((a0 - a2, a1 + a2, a2 - a1, a1 - a3))
+                raw = jnp.dot(lhs, wp[:, column : column + CH], preferred_element_type=f32)
+                for q in range(0, Q, 16):
+                    active = []
+                    for f in range(4):
+                        value = raw[f * Q + q : f * Q + q + 16] + bias_first
+                        if f >= 2:
+                            skip[f - 2, b, line, q : q + 16] = value.astype(bf16)
+                        power = jnp.mean(value * value, axis=1, keepdims=True)
+                        factor = lax.rsqrt(power + norm_eps) * (earlier if f < 2 else own)
+                        half = value * factor * half_gain
+                        active.append(half * jnp.tanh(half) + half)
+                    a0, a1, a2, a3 = active
+                    for k, value in enumerate((a0 - a2, a1 + a2, a2 - a1, a1 - a3)):
+                        turned[a, k, b, 8 + q : 24 + q] = value
             for k in range(4):
-                even, odd = sides[0][k], sides[1][k]
-                comps[4 * k, line] = (moved_down(odd) - odd).astype(bf16)
-                comps[4 * k + 1, line] = (even + odd).astype(bf16)
-                comps[4 * k + 2, line] = (odd - even).astype(bf16)
-                comps[4 * k + 3, line] = (even - moved_up(even)).astype(bf16)
-        return 0
-
-    for p in range(4):
-        patch_row(p, 0)
+                for q in range(0, Q, 16):
+                    even, odd = turned[a, k, 0, 8 + q : 24 + q], turned[a, k, 1, 8 + q : 24 + q]
+                    before, after = turned[a, k, 1, 7 + q : 23 + q], turned[a, k, 0, 9 + q : 25 + q]
+                    for c, value in enumerate((before - odd, even + odd, odd - even, even - after)):
+                        comps[4 * k + c, line, q : q + 16] = value.astype(bf16)
 
     def finish(f, b, n, middle):
         cols = slice(n * 256, (n + 1) * 256)
@@ -286,34 +281,71 @@
                 fine[f, r, 3, :, cols] = (odd - even).astype(bf16)
                 fine[f, r, 4, :, cols] = (moved_up(even) - odd).astype(bf16)
 
-    def phase_weights(a):
-        both = (wu.at[1], wu.at[2]) if a == 0 else (wu.at[0], wu.at[1])
-        alone = wu.at[2 * a]
-        wrow[...] = both[0][...] + both[1][...]
-        for i in range(2):
-            held = alone if i == a else wrow
-            k0, k1, k2 = [held[k * CH : (k + 1) * CH] for k in range(3)]
-            for n, value in enumerate((k0, k0 + k1 + k2, k2)):
-                wphase[a, n, i] = value
-
-    for k in range(4):
-        if k == 0:
-            mids[0].wait()
+    def rows_of(ref, at):
+        return ref[at : at + 16].astype(f32)
+
+    def mix_outer(i, slot):
+        for j in range(3):
+            for r in range(0, CH, 16):
+                left, centre, right = [rows_of(wm.at[i, j], m * CH + r) for m in range(3)]
+                ends = left + right
+                mixed[slot, 0, j * CH + r : j * CH + r + 16] = (ends + centre).astype(bf16)
+                mixed[slot, 1, j * CH + r : j * CH + r + 16] = (ends - centre).astype(bf16)
+
+    places = {
+        (1, 0): (0, 0), (1, 1): (0, 1), (1, 2): (0, 2), (1, 3): (1, 0),
+        (2, 0): (1, 1), (2, 1): (1, 2), (2, 2): (2, 1),
+    }
+
+    def mix_inner():
+        for j in range(3):
+            for r in range(0, CH, 16):
+                taps = [[rows_of(wm.at[i, j], m * CH + r) for m in range(3)] for i in range(3)]
+                sums, differences = [], []
+                for m in range(3):
+                    ends = taps[0][m] + taps[2][m]
+                    sums.append(ends + taps[1][m])
+                    differences.append(ends - taps[1][m])
+                for k, (left, centre, right) in ((1, sums), (2, differences)):
+                    ends = left + right
+                    for c, value in enumerate((left, ends + centre, ends - centre, right)):
+                        if (k, c) in places:
+                            i, m = places[k, c]
+                            wm[i, j, m * CH + r : m * CH + r + 16] = value.astype(bf16)
+                        else:
+                            last[j * CH + r : j * CH + r + 16] = value.astype(bf16)
+
+    def phase_weights(start):
+        for r in range(start, start + CH // 2, 16):
+            taps = [[rows_of(wu.at[j], m * CH + r) for m in range(3)] for j in range(3)]
+            low = [taps[0][m] + taps[1][m] for m in range(3)]
+            high = [taps[1][m] + taps[2][m] for m in range(3)]
+            for a, i, (left, centre, right) in (
+                (0, 0, taps[0]), (0, 1, high), (1, 0, low), (1, 1, taps[2])
+            ):
+                for n, value in enumerate((left, left + centre + right, right)):
+                    wphase[a, n, i, r : r + 16] = value.astype(bf16)
+
+    def middle_weights(k, c, cols):
+        if k in (0, 3) and c in (1, 2):
+            return mixed[k // 3, c - 1, :, cols]
+        if (k, c) == (2, 3):
+            return last[:, cols]
+        i, m = places[k, c] if k in (1, 2) else (2 * (k // 3), 2 * (c // 3))
+        return wm[i, :, m * CH : (m + 1) * CH, cols].reshape(3 * CH, 256)
+
+    for load in mids:
+        load.wait()
+    mix_outer(0, 0)
+    mix_outer(2, 1)
+    for k in (0, 3, 1, 2):
+        if k == 3:
+            mix_inner()
         if k == 1:
-            mids[1].wait()
-            mids[2].wait()
             up_load.wait()
-        if k > 1:
-            phase_weights(k - 2)
-        source = wm.at[0] if k == 0 else wm.at[2] if k == 3 else staged
-        if k in (1, 2):
-            for j in range(3):
-                ends = wm[0, j] + wm[2, j]
-                staged[j] = ends + wm[1, j] if k == 1 else ends - wm[1, j]
-        for j in range(3):
-            left, centre, right = [source[j, c * CH : (c + 1) * CH] for c in range(3)]
-            mixed[0, j * CH : (j + 1) * CH] = left + right + centre
-            mixed[1, j * CH : (j + 1) * CH] = left + right - centre
+            phase_weights(0)
+        if k == 2:
+            phase_weights(CH // 2)
         for n in range(2):
             cols = slice(n * 256, (n + 1) * 256)
             products = []
@@ -321,26 +353,19 @@
                 lhs = jnp.concatenate(
                     [comps[4 * k + c, j : j + 6].reshape(6 * Q, CH) for j in range(3)], axis=1
                 )
-                if c in (1, 2):
-                    rhs = mixed[c - 1, :, cols]
-                else:
-                    at = 0 if c == 0 else 2 * CH
-                    rhs = jnp.concatenate(
-                        [source[j, at : at + CH, cols] for j in range(3)], axis=0
-                    )
-                products.append(jnp.dot(lhs, rhs, preferred_element_type=f32))
+                products.append(
+                    jnp.dot(lhs, middle_weights(k, c, cols), preferred_element_type=f32)
+                )
             m0, m1, m2, m3 = products
             for b, total in enumerate((m0 + 0.5 * (m1 + m2), 0.5 * (m1 - m2) - m3)):
-                if k == 0:
-                    pending[0, b, :, cols] = total
+                if k in (0, 3):
+                    pending[k // 3, b, :, cols] = total
                 elif k == 1:
-                    pending[1, b, :, cols] = total
-                elif k == 2:
-                    held = pending[1, b, :, cols]
-                    pending[1, b, :, cols] = 0.5 * (held - total)
-                    finish(0, b, n, pending[0, b, :, cols] + 0.5 * (held + total))
+                    pending[0, b, :, cols] = pending[0, b, :, cols] + 0.5 * total
+                    pending[1, b, :, cols] = 0.5 * total - pending[1, b, :, cols]
                 else:
-                    finish(1, b, n, pending[1, b, :, cols] - total)
+                    finish(0, b, n, pending[0, b, :, cols] + 0.5 * total)
+                    finish(1, b, n, pending[1, b, :, cols] - 0.5 * total)
 
     writes = []
 
@@ -401,14 +426,14 @@
     dma = pltpu.SemaphoreType.DMA
     windows = pl.pallas_call(
         latent_kernel,
-        out_shape=jax.ShapeDtypeStruct((4, 6, Q, 256), bf16),
+        out_shape=jax.ShapeDtypeStruct((4, 4, Q, 256), bf16),
         in_specs=[anywhere] * 7,
         out_specs=vmem,
         scratch_shapes=[
-            pltpu.VMEM((8 * Q + 16, 4096), bf16),
+            pltpu.VMEM((8 * Q, 4096), bf16),
             pltpu.VMEM((64, 4096), bf16),
             pltpu.VMEM((2, 4096), f32),
-            pltpu.VMEM((128, 4096), bf16),
+            pltpu.VMEM((64, 4096), bf16),
             pltpu.VMEM((1, 64), f32),
             pltpu.VMEM((2, 1, 1), f32),
             pltpu.VMEM((2, 2, 2, 16, 128), f32),
@@ -439,11 +464,11 @@
             pltpu.VMEM((3, 3 * CH, CH), bf16),
             pltpu.VMEM((16, 8, Q, CH), bf16),
             pltpu.VMEM((2, 2, 8, Q, CH), bf16),
-            pltpu.VMEM((3, 3 * CH, CH), bf16),
-            pltpu.VMEM((2, 3 * CH, CH), bf16),
+            pltpu.VMEM((2, 4, 2, Q + 16, CH), f32),
+            pltpu.VMEM((2, 2, 3 * CH, CH), bf16),
+            pltpu.VMEM((3 * CH, CH), bf16),
             pltpu.VMEM((2, 2, 6 * Q, CH), f32),
             pltpu.VMEM((2, 6, 5, Q, CH), bf16),
-            pltpu.VMEM((3 * CH, CH), bf16),
             pltpu.VMEM((2, 3, 2, CH, CH), bf16),
             pltpu.VMEM((2, 4, 4, 256, 128), f32),
             dma, dma, dma((4,)), dma((3,)), dma, dma((16,)),

time: 42.6 us -> 44.9 us (1.054)
  Pallas kernels: 40.9 us -> 43.3 us
    pallas_call x1, Pallas kernels: 26.6 us -> 29.1 us  [on_device(): pl.pallas_call(decoder_kernel, out_shape=jax.ShapeDtypeStruct((2, 4, 2, 4...]
where the time goes in v5:
time: 44.9 us; the launch traced here: 44.8 us
  Pallas kernels  43.3 us (96%)
  between operations  1.49 us (3%)
    pallas_call x1, Pallas kernels, on_device(): pl.pallas_call(decoder_kernel, out_shape=jax.ShapeDtypeStruct((2, 4, 2, 4...  29.1 us
    pallas_call x1, Pallas kernels, on_device(): pl.pallas_call(latent_kernel, out_shape=jax.ShapeDtypeStruct((4, 4, Q, 25...  14.2 us

profile of v5, /device:TPU:96, one launch (start us, length us, event | category | flops | bytes accessed | tf_op | source)
XLA Modules:
  0.0 44.8 jit_solution(6762668301155739755)
XLA Ops:
  1.3 14.2 %shard_map.136.windows_ref = bf16[4,4,64,256]{3,2,1,0:T(8,128)(2,1)} custom-call(bf16[2,4,64,4096]{3,2,1,0:T(8,128)(2,1)} %h_ref.1, f32[2,4096]{1,0:T(2,128)} %mod_ref.1, bf16[64,4096]{1,0:T(8,128)(2,1)} %bitcast.12, f32[1,64]{1,0:T(1,128)} %bitcast.18, f32[1,1]{1,0:T(1,128)} %bitcast.10.g_ref, f32[1,1]{1,0:T(1,128)} %bitcast.11.sigma_ref, ...), custom_call_target="tpu_custom_call" | custom-call | tf_op jit(solution)/shard_map/pallas_call | solution.py:427
  15.5 29.1 %shard_map.137 = bf16[2,4,2,4,64,512]{5,4,3,2,1,0:T(8,128)(2,1)} custom-call(bf16[4,4,64,256]{3,2,1,0:T(8,128)(2,1)} %shard_map.136.windows_ref, bf16[3,3,48,512]{3,2,1,0:T(8,128)(2,1)} %win_ref.1, f32[1,512]{1,0:T(1,128)} %bitcast.14, f32[1,512]{1,0:T(1,128)} %bitcast.15, bf16[3,3,1536,512]{3,2,1,0:T(8,128)(2,1)} %wmid_ref.1, f32[1,512]{1,0:T(1,128)} %bitcast.16, ...), custom_call_target="tpu_custom_call" | custom-call | tf_op jit(solution)/shard_map/pallas_call | solution.py:453

commit v6 on v5

--- a/solution.py
+++ b/solution.py
@@ -282,15 +282,15 @@
                 fine[f, r, 4, :, cols] = (moved_up(even) - odd).astype(bf16)
 
     def rows_of(ref, at):
-        return ref[at : at + 16].astype(f32)
+        return ref[at : at + 16]
 
     def mix_outer(i, slot):
         for j in range(3):
             for r in range(0, CH, 16):
                 left, centre, right = [rows_of(wm.at[i, j], m * CH + r) for m in range(3)]
                 ends = left + right
-                mixed[slot, 0, j * CH + r : j * CH + r + 16] = (ends + centre).astype(bf16)
-                mixed[slot, 1, j * CH + r : j * CH + r + 16] = (ends - centre).astype(bf16)
+                mixed[slot, 0, j * CH + r : j * CH + r + 16] = ends + centre
+                mixed[slot, 1, j * CH + r : j * CH + r + 16] = ends - centre
 
     places = {
         (1, 0): (0, 0), (1, 1): (0, 1), (1, 2): (0, 2), (1, 3): (1, 0),
@@ -311,9 +311,9 @@
                     for c, value in enumerate((left, ends + centre, ends - centre, right)):
                         if (k, c) in places:
                             i, m = places[k, c]
-                            wm[i, j, m * CH + r : m * CH + r + 16] = value.astype(bf16)
+                            wm[i, j, m * CH + r : m * CH + r + 16] = value
                         else:
-                            last[j * CH + r : j * CH + r + 16] = value.astype(bf16)
+                            last[j * CH + r : j * CH + r + 16] = value
 
     def phase_weights(start):
         for r in range(start, start + CH // 2, 16):
@@ -324,7 +324,7 @@
                 (0, 0, taps[0]), (0, 1, high), (1, 0, low), (1, 1, taps[2])
             ):
                 for n, value in enumerate((left, left + centre + right, right)):
-                    wphase[a, n, i, r : r + 16] = value.astype(bf16)
+                    wphase[a, n, i, r : r + 16] = value
 
     def middle_weights(k, c, cols):
         if k in (0, 3) and c in (1, 2):
@@ -334,12 +334,13 @@
         i, m = places[k, c] if k in (1, 2) else (2 * (k // 3), 2 * (c // 3))
         return wm[i, :, m * CH : (m + 1) * CH, cols].reshape(3 * CH, 256)
 
-    for load in mids:
-        load.wait()
+    mids[0].wait()
     mix_outer(0, 0)
-    mix_outer(2, 1)
     for k in (0, 3, 1, 2):
         if k == 3:
+            mids[1].wait()
+            mids[2].wait()
+            mix_outer(2, 1)
             mix_inner()
         if k == 1:
             up_load.wait()

time: 44.9 us -> 43.3 us (0.964)
  Pallas kernels: 43.3 us -> 41.6 us
    pallas_call x1, Pallas kernels: 29.1 us -> 27.4 us  [on_device(): pl.pallas_call(decoder_kernel, out_shape=jax.ShapeDtypeStruct((2, 4, 2, 4...]
where the time goes in v6:
time: 43.3 us; the launch traced here: 43.1 us
  Pallas kernels  41.6 us (96%)
  between operations  1.49 us (3%)
    pallas_call x1, Pallas kernels, on_device(): pl.pallas_call(decoder_kernel, out_shape=jax.ShapeDtypeStruct((2, 4, 2, 4...  27.4 us
    pallas_call x1, Pallas kernels, on_device(): pl.pallas_call(latent_kernel, out_shape=jax.ShapeDtypeStruct((4, 4, Q, 25...  14.2 us

profile of v6, /device:TPU:96, one launch (start us, length us, event | category | flops | bytes accessed | tf_op | source)
XLA Modules:
  0.0 43.1 jit_solution(16062118435035652435)
XLA Ops:
  1.3 14.2 %shard_map.136.windows_ref = bf16[4,4,64,256]{3,2,1,0:T(8,128)(2,1)} custom-call(bf16[2,4,64,4096]{3,2,1,0:T(8,128)(2,1)} %h_ref.1, f32[2,4096]{1,0:T(2,128)} %mod_ref.1, bf16[64,4096]{1,0:T(8,128)(2,1)} %bitcast.12, f32[1,64]{1,0:T(1,128)} %bitcast.18, f32[1,1]{1,0:T(1,128)} %bitcast.10.g_ref, f32[1,1]{1,0:T(1,128)} %bitcast.11.sigma_ref, ...), custom_call_target="tpu_custom_call" | custom-call | tf_op jit(solution)/shard_map/pallas_call | solution.py:428
  15.5 27.4 %shard_map.137 = bf16[2,4,2,4,64,512]{5,4,3,2,1,0:T(8,128)(2,1)} custom-call(bf16[4,4,64,256]{3,2,1,0:T(8,128)(2,1)} %shard_map.136.windows_ref, bf16[3,3,48,512]{3,2,1,0:T(8,128)(2,1)} %win_ref.1, f32[1,512]{1,0:T(1,128)} %bitcast.14, f32[1,512]{1,0:T(1,128)} %bitcast.15, bf16[3,3,1536,512]{3,2,1,0:T(8,128)(2,1)} %wmid_ref.1, f32[1,512]{1,0:T(1,128)} %bitcast.16, ...), custom_call_target="tpu_custom_call" | custom-call | tf_op jit(solution)/shard_map/pallas_call | solution.py:454

commit v7 on v4

--- a/solution.py
+++ b/solution.py
@@ -73,29 +73,24 @@
 
     for load in small:
         load.wait()
-    scale = 1.0 + mod[1:2, :]
-    shift = mod[0:1, :]
-    for n, block in enumerate((0, 2, 1, 3)):
-        part = wbuf[block * 16 : block * 16 + 16]
-        wmat[n * 16 : n * 16 + 16] = (part.astype(f32) * scale).astype(bf16)
-        wmat[64 + n * 16 : 80 + n * 16] = part
-    shift_hi = shift.astype(bf16)
-    shift_lo = (shift - shift_hi.astype(f32)).astype(bf16)
-    row = lax.broadcasted_iota(jnp.int32, (16, shift.shape[1]), 0)
-    hbuf[8 * Q :] = jnp.where(
-        row == 0,
-        1.0,
-        jnp.where(
-            row == 1, shift_hi.astype(f32), jnp.where(row == 2, shift_lo.astype(f32), 0.0)
-        ),
-    ).astype(bf16)
-    lane = lax.broadcasted_iota(jnp.int32, (Q, Q), 1)
-    source = ((lane // 16) % 2) * 32 + (lane // 32) * 16 + lane % 16
-    one_hot = (lax.broadcasted_iota(jnp.int32, (Q, Q), 0) == source).astype(f32)
-    bias = jnp.dot(
-        jnp.broadcast_to(bias_in[...], (8, Q)), one_hot,
-        preferred_element_type=f32, precision=lax.Precision.HIGHEST,
-    )[0:1]
+    scale, shift = 1.0 + mod[1:2, :], mod[0:1, :]
+    scaled_sum, shift_sum = jnp.zeros((Q, 128), f32), jnp.zeros((Q, 128), f32)
+    for k in range(32):
+        at = slice(k * 128, (k + 1) * 128)
+        plain = jnp.concatenate(
+            [wbuf[n * 16 : n * 16 + 16, at].astype(f32) for n in (0, 2, 1, 3)], axis=0
+        )
+        scaled = (plain * scale[:, at]).astype(bf16)
+        wmat[:, at] = scaled
+        scaled_sum = scaled_sum + scaled.astype(f32)
+        shift_sum = shift_sum + plain * shift[:, at]
+    totals = jnp.sum(
+        jnp.transpose(jnp.concatenate([scaled_sum, shift_sum], axis=0)), axis=0, keepdims=True
+    )
+    bias = jnp.concatenate(
+        [bias_in[:, n * 16 : n * 16 + 16] for n in (0, 2, 1, 3)], axis=1
+    )
+    column_sum, constant = totals[:, :Q], totals[:, Q:] + bias
     guidance, sigma = scalars[0], scalars[1]
 
     for load in loads:
@@ -113,12 +108,10 @@
         offset = jnp.sum(first, axis=1, keepdims=True) * (1.0 / 4096)
         spread = jnp.sum(second, axis=1, keepdims=True) * (1.0 / 4096) - offset * offset
         statistics.append((pivot + offset, lax.rsqrt(jnp.maximum(spread, 0.0) + norm_eps)))
-    column_sum = product[8 * Q : 8 * Q + 1, :Q]
-    constant = product[8 * Q + 1 : 8 * Q + 2, Q:] + product[8 * Q + 2 : 8 * Q + 3, Q:] + bias
     predictions = []
     for f in range(4):
         centre, inverse = statistics[f]
-        branch = inverse * (product[2 * f * Q : 2 * (f + 1) * Q, :Q] - centre * column_sum)
+        branch = inverse * (product[2 * f * Q : 2 * (f + 1) * Q] - centre * column_sum)
         cond, uncond = branch[:Q], branch[Q:]
         predictions.append(uncond + guidance * (cond - uncond) + constant)
 
@@ -193,12 +186,11 @@
         jnp.concatenate(parts, axis=0), widen, preferred_element_type=f32
     ).astype(bf16).reshape(6, 2, Q, 256)
     for p in range(4):
-        windows[p, 0:2] = jnp.zeros((2, Q, 256), bf16)
         for f in range(2, 6):
             at = slice(f % 2 * 128, f % 2 * 128 + 128)
             above, own, below = [wide[p + k, f // 2 - 1, :, at] for k in range(3)]
             beside = jnp.where(wide_lane < 64, below.astype(f32), above.astype(f32)).astype(bf16)
-            windows[p, f] = jnp.concatenate([own, beside], axis=1)
+            windows[p, f - 2] = jnp.concatenate([own, beside], axis=1)
 
 
 def decoder_kernel(
@@ -209,7 +201,8 @@
     s, t = lax.axis_index("space"), lax.axis_index("tm")
     ns = lax.axis_size("space")
     others = [
-        pltpu.make_async_copy(windows_ref, windows, lsem), pltpu.make_async_copy(win_ref, win, wsem)
+        pltpu.make_async_copy(windows_ref, windows.at[:, 2:6], lsem),
+        pltpu.make_async_copy(win_ref, win, wsem),
     ]
     for n, ref in enumerate((bin_ref, gain_ref, bmid_ref, bup_ref)):
         others.append(pltpu.make_async_copy(ref, vectors.at[n], vsem.at[n]))
@@ -217,6 +210,7 @@
         load.start()
 
     wp[...] = jnp.zeros(wp.shape, bf16)
+    windows[:, 0:2] = jnp.zeros((4, 2, Q, 256), bf16)
     for load in others:
         load.wait()
     mids = [pltpu.make_async_copy(wmid_ref.at[i], wm.at[i], msem.at[i]) for i in range(3)]
@@ -312,8 +306,8 @@
                 staged[j] = ends + wm[1, j] if k == 1 else ends - wm[1, j]
         for j in range(3):
             left, centre, right = [source[j, c * CH : (c + 1) * CH] for c in range(3)]
-            mixed[0, j * CH : (j + 1) * CH] = left + right + centre
-            mixed[1, j * CH : (j + 1) * CH] = left + right - centre
+            mixed[k % 2, 0, j * CH : (j + 1) * CH] = left + right + centre
+            mixed[k % 2, 1, j * CH : (j + 1) * CH] = left + right - centre
         for n in range(2):
             cols = slice(n * 256, (n + 1) * 256)
             products = []
@@ -322,7 +316,7 @@
                     [comps[4 * k + c, j : j + 6].reshape(6 * Q, CH) for j in range(3)], axis=1
                 )
                 if c in (1, 2):
-                    rhs = mixed[c - 1, :, cols]
+                    rhs = mixed[k % 2, c - 1, :, cols]
                 else:
                     at = 0 if c == 0 else 2 * CH
                     rhs = jnp.concatenate(
@@ -348,7 +342,7 @@
         for r in range(4):
             line = 8 * a + 4 * f + r
             for g in range(4):
-                comps[line, 0:4, :, g * 128 : (g + 1) * 128] = stage[f, r, g].astype(bf16).reshape(
+                comps[line, 0:4, :, g * 128 : (g + 1) * 128] = stage[a, r, g].astype(bf16).reshape(
                     4, Q, 128
                 )
             write = pltpu.make_async_copy(
@@ -358,8 +352,8 @@
             writes.append(write)
 
     behind = None
-    for a in range(2):
-        for f in range(2):
+    for f in range(2):
+        for a in range(2):
             for n in range(2):
                 cols = slice(n * 256, (n + 1) * 256)
                 products = []
@@ -380,7 +374,7 @@
                         for side in range(2):
                             at = (2 * r + side) * Q
                             for g in range(2):
-                                stage[f, r, 2 * n + g, pl.ds(2 * side + b, Q, stride=4), :] = value[
+                                stage[a, r, 2 * n + g, pl.ds(2 * side + b, Q, stride=4), :] = value[
                                     at : at + Q, g * 128 : (g + 1) * 128
                                 ]
             if behind is not None:
@@ -401,14 +395,14 @@
     dma = pltpu.SemaphoreType.DMA
     windows = pl.pallas_call(
         latent_kernel,
-        out_shape=jax.ShapeDtypeStruct((4, 6, Q, 256), bf16),
+        out_shape=jax.ShapeDtypeStruct((4, 4, Q, 256), bf16),
         in_specs=[anywhere] * 7,
         out_specs=vmem,
         scratch_shapes=[
-            pltpu.VMEM((8 * Q + 16, 4096), bf16),
+            pltpu.VMEM((8 * Q, 4096), bf16),
             pltpu.VMEM((64, 4096), bf16),
             pltpu.VMEM((2, 4096), f32),
-            pltpu.VMEM((128, 4096), bf16),
+            pltpu.VMEM((64, 4096), bf16),
             pltpu.VMEM((1, 64), f32),
             pltpu.VMEM((2, 1, 1), f32),
             pltpu.VMEM((2, 2, 2, 16, 128), f32),
@@ -440,7 +434,7 @@
             pltpu.VMEM((16, 8, Q, CH), bf16),
             pltpu.VMEM((2, 2, 8, Q, CH), bf16),
             pltpu.VMEM((3, 3 * CH, CH), bf16),
-            pltpu.VMEM((2, 3 * CH, CH), bf16),
+            pltpu.VMEM((2, 2, 3 * CH, CH), bf16),
             pltpu.VMEM((2, 2, 6 * Q, CH), f32),
             pltpu.VMEM((2, 6, 5, Q, CH), bf16),
             pltpu.VMEM((3 * CH, CH), bf16),

time: 42.6 us -> 42.4 us (level)
  no operation moved by 1% of the time
where the time goes in v7:
time: 42.4 us; the launch traced here: 42.2 us
  Pallas kernels  40.7 us (96%)
  between operations  1.49 us (4%)
    pallas_call x1, Pallas kernels, on_device(): pl.pallas_call(decoder_kernel, out_shape=jax.ShapeDtypeStruct((2, 4, 2, 4...  26.5 us
    pallas_call x1, Pallas kernels, on_device(): pl.pallas_call(latent_kernel, out_shape=jax.ShapeDtypeStruct((4, 4, Q, 25...  14.2 us

profile of v7, /device:TPU:96, one launch (start us, length us, event | category | flops | bytes accessed | tf_op | source)
XLA Modules:
  0.0 42.2 jit_solution(17596398831964091614)
XLA Ops:
  1.3 14.2 %shard_map.136.windows_ref = bf16[4,4,64,256]{3,2,1,0:T(8,128)(2,1)} custom-call(bf16[2,4,64,4096]{3,2,1,0:T(8,128)(2,1)} %h_ref.1, f32[2,4096]{1,0:T(2,128)} %mod_ref.1, bf16[64,4096]{1,0:T(8,128)(2,1)} %bitcast.12, f32[1,64]{1,0:T(1,128)} %bitcast.18, f32[1,1]{1,0:T(1,128)} %bitcast.10.g_ref, f32[1,1]{1,0:T(1,128)} %bitcast.11.sigma_ref, ...), custom_call_target="tpu_custom_call" | custom-call | tf_op jit(solution)/shard_map/pallas_call | solution.py:396
  15.5 26.5 %shard_map.137 = bf16[2,4,2,4,64,512]{5,4,3,2,1,0:T(8,128)(2,1)} custom-call(bf16[4,4,64,256]{3,2,1,0:T(8,128)(2,1)} %shard_map.136.windows_ref, bf16[3,3,48,512]{3,2,1,0:T(8,128)(2,1)} %win_ref.1, f32[1,512]{1,0:T(1,128)} %bitcast.14, f32[1,512]{1,0:T(1,128)} %bitcast.15, bf16[3,3,1536,512]{3,2,1,0:T(8,128)(2,1)} %wmid_ref.1, f32[1,512]{1,0:T(1,128)} %bitcast.16, ...), custom_call_target="tpu_custom_call" | custom-call | tf_op jit(solution)/shard_map/pallas_call | solution.py:422
